TPU v7x, 256 devices: a whole 4x4x8 slice. The times are simulated.
256 devices in a mesh: slab: 64 (over z, y, core), group: 4 (over x).
Axes of the slice: x: 4, y: 4, z: 8, core: 2. Of those that a mesh axis runs over, the one named last changes fastest.
Arguments:
- coarse: bfloat16 [4, 64, 4, 2, 64, 128], P('group', 'slab'), may hold values from -6 to 6
- tconv_weight: bfloat16 [3, 3, 3, 128, 64], replicated, may hold values from -0.3125 to 0.3125
- conv_weight: bfloat16 [3, 3, 3, 64, 64], replicated, may hold values from -0.15625 to 0.15625
- cotangent: bfloat16 [4, 64, 64, 8, 4, 128], P('group', 'slab'), may hold values from -6 to 6
Outputs:
- field: bfloat16 [4, 64, 64, 8, 4, 128], P('group', 'slab')
- grad_coarse: bfloat16 [4, 64, 4, 2, 64, 128], P('group', 'slab')
- grad_conv_weight: float32 [3, 3, 3, 64, 64], replicated
- grad_tconv_weight: float32 [3, 3, 3, 128, 64], replicated
All inputs are finite; a program needn't handle non-finite values.
Results may differ from a plain program's by a relative error of at most 0.009.
Values may be sent and summed in bfloat16 or wider, within the bound.
A program may use at most 64 MiB of HBM per device.

v0:
```python
import jax
import jax.numpy as jnp
from jax import lax
from jax.sharding import PartitionSpec as P

PY = 4


def passed_along(block, axis, distance):
    devices = range(lax.axis_size(axis))
    route = [(i - distance, i) for i in devices if i - distance in devices]
    return lax.ppermute(block, axis, route)


def as_sent(x):
    return jax.tree.map(lambda a: a.astype(jnp.bfloat16) if a.dtype == jnp.float32 else a, x)


def convolve(
    left, right, strides, padding, spec, input_dilation=(1, 1, 1), kernel_dilation=(1, 1, 1)
):
    return lax.conv_general_dilated(
        left,
        right,
        strides,
        padding,
        lhs_dilation=input_dilation,
        rhs_dilation=kernel_dilation,
        dimension_numbers=spec,
        preferred_element_type=jnp.float32,
    )


def masked(keep, values):
    return jnp.where(keep, values, jnp.zeros_like(values))


def per_device(coarse, tconv_weight, conv_weight, cotangent):
    spec_up = ("NDHWC", "DHWIO", "NCDHW")
    spec_fine = ("NCDHW", "DHWIO", "NCDHW")
    lane = lax.axis_index("slab") % PY
    has_below = lane != 0
    has_above = lane != PY - 1
    local_coarse = coarse[0]
    local_grad = cotangent[0]
    flipped = tconv_weight[::-1, ::-1, ::-1]
    partial_planes = convolve(
        local_coarse,
        flipped,
        (1, 1, 1),
        [(2, 2), (2, 2), (1, 2)],
        spec_up,
        input_dilation=(2, 2, 2),
    )
    row_spill = masked(
        has_above,
        passed_along(partial_planes[:, :, :, 0:1].astype(jnp.bfloat16), "slab", -1).astype(
            jnp.float32
        ),
    )
    trimmed = partial_planes[:, :, :, 1:]
    trimmed = jnp.concatenate([trimmed[:, :, :, :-1], trimmed[:, :, :, -1:] + row_spill], axis=3)
    plane_spill = passed_along(as_sent(trimmed[:, :, 0:1]), "slab", -PY)
    rest = trimmed[:, :, 1:]
    hidden = jnp.concatenate([rest[:, :, :-1], rest[:, :, -1:] + plane_spill], axis=2)
    squash = jax.nn.sigmoid(hidden)
    active = (hidden * squash).astype(jnp.bfloat16)
    stacked = jnp.concatenate([active, local_grad], axis=0)
    rims = []
    for step_by, keep in ((1, has_below), (-1, has_above)):
        edge_row = stacked[:, :, :, -1:] if step_by > 0 else stacked[:, :, :, :1]
        arrived = passed_along(edge_row, "slab", step_by)
        rims.append(masked(keep, arrived))
    wide = jnp.concatenate([rims[0], stacked, rims[1]], axis=3)
    planes = []
    for step_by in (PY, -PY):
        edge_plane = wide[:, :, -1:] if step_by > 0 else wide[:, :, :1]
        planes.append(passed_along(edge_plane, "slab", step_by))
    padded_pair = jnp.concatenate([planes[0], wide, planes[1]], axis=2)
    padded = padded_pair[0:1]
    grad_padded = padded_pair[1:2]
    field = convolve(padded, conv_weight, (1, 1, 1), [(0, 0), (0, 0), (1, 1)], spec_fine).astype(
        jnp.bfloat16
    )
    back_kernel = jnp.swapaxes(conv_weight[::-1, ::-1, ::-1], 3, 4)
    grad_active = convolve(grad_padded, back_kernel, (1, 1, 1), [(0, 0), (0, 0), (1, 1)], spec_fine)
    conv_local = convolve(
        padded, local_grad, (1, 1, 1), [(0, 0), (0, 0), (1, 1)], ("CNDHW", "IODHW", "NCDHW")
    )
    conv_local = jnp.transpose(conv_local, (2, 3, 4, 0, 1))
    grad_hidden = (grad_active * squash * (1.0 + hidden * (1.0 - squash))).astype(jnp.bfloat16)
    conv_total = lax.psum(conv_local, ("slab", "group"))
    low_row = masked(has_below, passed_along(grad_hidden[:, :, :, -1:], "slab", 1))
    grad_rows = jnp.concatenate([low_row, grad_hidden], axis=3)
    low_plane = passed_along(grad_rows[:, :, -1:], "slab", PY)
    grad_ext = jnp.concatenate([low_plane, grad_rows], axis=2)
    grad_coarse = convolve(
        grad_ext,
        jnp.swapaxes(tconv_weight, 3, 4),
        (2, 2, 2),
        [(0, 0), (0, 0), (1, 0)],
        ("NCDHW", "DHWIO", "NDHWC"),
    ).astype(jnp.bfloat16)
    tconv_local = convolve(
        grad_ext,
        local_coarse,
        (1, 1, 1),
        [(0, 0), (0, 0), (1, 0)],
        ("CNDHW", "IDHWO", "NCDHW"),
        kernel_dilation=(2, 2, 2),
    )
    tconv_local = jnp.transpose(tconv_local, (2, 3, 4, 1, 0))
    tconv_total = lax.psum(tconv_local, ("slab", "group"))
    devices = lax.axis_size("slab") * lax.axis_size("group")
    fine_cells = devices * local_grad.shape[2] * local_grad.shape[3] * local_grad.shape[4]
    coarse_cells = devices * local_coarse.shape[1] * local_coarse.shape[2] * local_coarse.shape[3]
    grad_conv_weight = conv_total / jnp.sqrt(jnp.float32(fine_cells))
    grad_tconv_weight = tconv_total / jnp.sqrt(jnp.float32(coarse_cells))
    return (field[None], grad_coarse[None], grad_conv_weight, grad_tconv_weight)


def solution(mesh):
    return jax.shard_map(
        per_device,
        mesh=mesh,
        in_specs=(
            P("group", "slab", None, None, None, None),
            P(),
            P(),
            P("group", "slab", None, None, None, None),
        ),
        out_specs=(
            P("group", "slab", None, None, None, None),
            P("group", "slab", None, None, None, None),
            P(),
            P(),
        ),
        check_vma=False,
    )
```

profile of v0, /device:TPU:2, one launch (start us, length us, event | category | flops | bytes accessed | tf_op | source)
XLA Modules:
  0.0 460.4 jit_solution(9557490093788269804)
XLA Ops:
  7.2 1.1 copy.145
  8.5 3.6 convolution_select_fusion
  12.1 1.7 copy-done.1
  14.3 1.3 collective-permute-start
  15.6 2.1 copy.159
  17.7 0.7 copy.114
  18.4 1.3 copy.143
  19.7 1.9 copy.112
  21.6 2.4 reshape.177
  24.0 1.5 slice.79
  25.5 3.1 copy.142
  28.9 1.3 collective-permute-start.1
  30.3 8.5 %collective-permute-done.1 = bf16[1,64,1,4,128]{4,2,3,1,0:T(2,128)(2,1)S(1)} collective-permute-done((bf16[1,64,1,4,128]{4,2,3,1,0:T(2,128)(2,1)S(1)}, bf16[1,64,1,4,128]{4,2,3,1,0:T(2,128)(2,1)S(1)}, u32[]{:S(2)}, u32[]{:S(2)}) %collective-permute-start.1) | collective-permute-done | bytes 65568 | tf_op jit(solution)/shard_map/ppermute | solution.py:12
  39.0 0.4 multiply_convert_fusion
  39.4 1.3 collective-permute-start.3
  40.7 3.0 collective-permute-start.2
  43.8 1.1 collective-permute-done.2
  45.0 0.7 pad_maximum_fusion.5
  45.7 1.3 collective-permute-start.5
  47.0 11.5 %collective-permute-start.4 = (bf16[2,64,1,6,128]{4,2,3,1,0:T(2,128)(2,1)S(1)}, bf16[2,64,1,6,128]{4,2,3,1,0:T(2,128)(2,1)}, u32[]{:S(2)}, u32[]{:S(2)}) collective-permute-start(bf16[2,64,1,6,128]{4,2,3,1,0:T(2,128)(2,1)S(1)} %get-tuple-element.24), channel_id=1, source_target_pairs={{0,16},{4,20},{8,24},{12,28},{16,32},{20,36},{24,40},{28,44},{32,4... | collective-permute-start | bytes 589832 | tf_op jit(solution)/shard_map/ppermute | solution.py:12
  58.5 2.6 copy.137
  61.1 3.1 collective-permute-done.5
  64.2 8.5 %collective-permute-done.4 = bf16[2,64,1,6,128]{4,2,3,1,0:T(2,128)(2,1)} collective-permute-done((bf16[2,64,1,6,128]{4,2,3,1,0:T(2,128)(2,1)S(1)}, bf16[2,64,1,6,128]{4,2,3,1,0:T(2,128)(2,1)}, u32[]{:S(2)}, u32[]{:S(2)}) %collective-permute-start.4) | collective-permute-done | bytes 196640 | tf_op jit(solution)/shard_map/ppermute | solution.py:12
  72.6 3.3 pad_maximum_fusion
  76.0 0.5 fusion.66
  76.5 0.4 copy.156
  76.9 1.8 copy.146
  78.8 3.6 pad.4.clone
  82.4 5.1 %reshape.164 = bf16[64,10,6,1,8,17]{0,5,4,2,1,3:T(8,128)(2,1)} reshape(bf16[64,10,6,1,136]{0,4,2,1,3:T(8,128)(2,1)} %pad.4.clone) | data formatting | bytes 2088960 | tf_op jit(solution)/shard_map/conv_general_dilated | solution.py:22
  87.5 2.2 copy.128
  89.8 8.6 %fusion.26 = f32[8,4,8,17,64]{4,2,3,1,0:T(8,128)S(1)} fusion(bf16[3,3,3,64,64]{4,3,2,1,0:T(8,128)(2,1)S(1)} %copy-done, bf16[64,10,6,1,7,2]{0,4,5,2,1,3:T(8,128)(2,1)S(1)} %slice.92, bf16[64,10,6,1,8,17]{0,4,5,2,1,3:T(8,128)(2,1)S(1)} %copy.128, pred[8,17]{0,1:T(8,128)(4,1)S(1)} %copy-done.13), kind=kOutput, calls=%fused_computation.30 | convolution fusion | flops 966373376 | bytes 2487432 | tf_op jit(solution)/shard_map/conv_general_dilated | solution.py:22
  98.4 1.3 copy.129
  99.7 1.5 slice.93
  101.2 3.7 copy.144
  104.8 1.7 fusion.39
  106.6 0.8 copy-done.7
  107.4 0.7 slice.94
  108.0 2.6 collective-permute-start.6
  110.6 6.9 %copy.136 = bf16[1,64,10,6,128]{1,0,4,3,2:T(2,128)(2,1)} copy(bf16[1,64,10,6,128]{4,2,3,1,0:T(8,128)(2,1)S(1)} %get-tuple-element.23) | data formatting | bytes 1966080 | tf_op jit(solution)/shard_map/slice | solution.py:80
  117.6 33.0 %fusion.67 = f32[3,3,3,64,64]{4,3,2,1,0:T(8,128)} fusion(bf16[1,64,10,6,128]{1,0,4,3,2:T(2,128)(2,1)} %copy.136, bf16[1,64,8,4,128]{1,0,4,3,2:T(2,128)(2,1)} %copy.137), kind=kOutput, calls=%fused_computation.92 | convolution fusion | flops 901251072 | bytes 1949696 | tf_op jit(solution)/shard_map/transpose | solution.py:90
  150.6 0.4 copy.157
  151.0 1.1 copy.147
  152.0 2.1 pad.2.clone
  154.1 3.6 reshape.157
  157.7 0.3 copy.123
  158.2 0.5 copy-done.8
  158.9 5.4 %collective-permute-start.7 = (bf16[1,64,1,5,128]{4,2,3,1,0:T(2,128)(2,1)S(1)}, bf16[1,64,1,5,128]{4,2,3,1,0:T(2,128)(2,1)S(1)}, u32[]{:S(2)}, u32[]{:S(2)}) collective-permute-start(bf16[1,64,1,5,128]{4,2,3,1,0:T(2,128)(2,1)S(1)} %pad_maximum_fusion.8), channel_id=1, source_target_pairs={{0,16},{4,20},{8,24},{12,28},{16,32},{20,36},{24,40},{28,44},{32,4... | collective-permute-start | bytes 245768 | tf_op jit(solution)/shard_map/ppermute | solution.py:12
  164.3 4.3 select_convert_fusion
  168.7 0.4 copy.124
  169.1 0.5 maximum_maximum_fusion
  169.6 5.8 %copy.138 = bf16[1,64,9,5,128]{1,0,4,3,2:T(2,128)(2,1)} copy(bf16[1,64,9,5,128]{4,2,3,1,0:T(8,128)(2,1)S(1)} %maximum_maximum_fusion) | data formatting | bytes 1474560 | tf_op jit(solution)/shard_map/concatenate | solution.py:96
  175.4 8.5 %fusion.42 = f32[3,3,3,128,64]{3,4,2,1,0:T(8,128)} fusion(bf16[1,64,9,5,128]{1,0,4,3,2:T(2,128)(2,1)} %copy.138, bf16[1,4,2,64,128]{4,3,2,1,0:T(8,128)(2,1)S(1)} %bitcast.93), kind=kOutput, calls=%fused_computation.64 | convolution fusion | flops 225312768 | bytes 1753088 | tf_op jit(solution)/shard_map/transpose | solution.py:112
  183.9 1.0 slice_bitcast_fusion
  184.9 3.1 copy.140
  188.2 1.4 copy.148
  189.7 1.7 pad.6.clone
  191.4 2.6 reshape.169
  194.0 0.2 copy.134
  194.3 0.7 copy-done.11
  195.0 0.8 fusion.34
  196.1 0.7 copy.141
  196.7 253.1 %all-reduce.3.cloned.1.call-done = (f32[3,3,3,64,64]{4,3,2,1,0:T(8,128)}, f32[3,3,3,128,64]{3,4,2,1,0:T(8,128)}) async-done(((f32[3,3,3,64,64]{4,3,2,1,0:T(8,128)}, f32[3,3,3,128,64]{3,4,2,1,0:T(8,128)}), (f32[3,3,3,64,64]{4,3,2,1,0:T(8,128)}, f32[3,3,3,128,64]{3,4,2,1,0:T(8,128)})) %all-reduce.3.cloned.1.call-update) | async-done | bytes 1327120 | tf_op jit(solution)/shard_map/psum | solution.py:92
  449.9 2.3 broadcast_multiply_fusion.1
  452.1 1.0 broadcast_multiply_fusion
  (62 shorter events, 2.2 us)
Async XLA Ops:
  7.2 82.6 %copy-start = (bf16[3,3,3,64,64]{4,3,2,1,0:T(8,128)(2,1)S(1)}, bf16[3,3,3,64,64]{4,3,2,1,0:T(8,128)(2,1)}, u32[]{:S(2)}) copy-start(bf16[3,3,3,64,64]{4,3,2,1,0:T(8,128)(2,1)} %param.6) | copy-start | bytes 663556
  7.2 442.7 %all-reduce.3.cloned.1.call-start = ((), (), s32[]{:S(2)}) async-start(), calls=%async_computation | async-start | bytes 3538944 | tf_op jit(solution)/shard_map/psum | solution.py:92
  12.1 1.7 copy-start.1
  14.3 14.4 %collective-permute-start = (bf16[1,64,9,1,128]{4,1,3,2,0:T(8,128)(2,1)S(1)}, bf16[1,64,9,1,128]{4,1,3,2,0:T(8,128)(2,1)S(1)}, u32[]{:S(2)}, u32[]{:S(2)}) collective-permute-start(bf16[1,64,9,1,128]{4,1,3,2,0:T(8,128)(2,1)S(1)} %copy.117), channel_id=1, source_target_pairs={{4,0},{8,4},{12,8},{16,12},{20,16},{24,20},{28,24},{32,28},{36,32}... | collective-permute-start | bytes 442376 | tf_op jit(solution)/shard_map/ppermute | solution.py:12
  15.6 2.1 slice-start
  15.6 4.1 slice-start.1
  25.5 3.2 copy-start.9
  28.9 9.9 %collective-permute-start.1 = (bf16[1,64,1,4,128]{4,2,3,1,0:T(2,128)(2,1)S(1)}, bf16[1,64,1,4,128]{4,2,3,1,0:T(2,128)(2,1)S(1)}, u32[]{:S(2)}, u32[]{:S(2)}) collective-permute-start(bf16[1,64,1,4,128]{4,2,3,1,0:T(2,128)(2,1)S(1)} %fusion.52), channel_id=1, source_target_pairs={{16,0},{20,4},{24,8},{28,12},{32,16},{36,20},{40,24},{44,28},{48,3... | collective-permute-start | bytes 196616 | tf_op jit(solution)/shard_map/ppermute | solution.py:12
  30.3 9.1 %copy-start.5 = (f32[1,64,7,4,128]{4,2,3,1,0:T(8,128)}, f32[1,64,7,4,128]{4,2,3,1,0:T(8,128)S(1)}, u32[]{:S(2)}) copy-start(f32[1,64,7,4,128]{4,2,3,1,0:T(8,128)S(1)} %fusion.37) | copy-start | bytes 2752516
  30.3 9.0 %copy-start.4 = (bf16[1,1,64,8,4,128]{5,3,4,2,1,0:T(8,128)(2,1)S(1)}, bf16[1,1,64,8,4,128]{5,3,4,2,1,0:T(8,128)(2,1)}, u32[]{:S(2)}) copy-start(bf16[1,1,64,8,4,128]{5,3,4,2,1,0:T(8,128)(2,1)} %copy.159) | copy-start | bytes 1572868
  39.4 4.4 collective-permute-start.3
  40.7 4.2 collective-permute-start.2
  45.7 18.5 %collective-permute-start.5 = (bf16[2,64,1,6,128]{4,2,3,1,0:T(2,128)(2,1)S(1)}, bf16[2,64,1,6,128]{4,2,3,1,0:T(2,128)(2,1)}, u32[]{:S(2)}, u32[]{:S(2)}) collective-permute-start(bf16[2,64,1,6,128]{4,2,3,1,0:T(2,128)(2,1)S(1)} %get-tuple-element.25), channel_id=1, source_target_pairs={{16,0},{20,4},{24,8},{28,12},{32,16},{36,20},{40,24},{44,28},{48,3... | collective-permute-start | bytes 589832 | tf_op jit(solution)/shard_map/ppermute | solution.py:12
  47.0 25.7 %collective-permute-start.4 = (bf16[2,64,1,6,128]{4,2,3,1,0:T(2,128)(2,1)S(1)}, bf16[2,64,1,6,128]{4,2,3,1,0:T(2,128)(2,1)}, u32[]{:S(2)}, u32[]{:S(2)}) collective-permute-start(bf16[2,64,1,6,128]{4,2,3,1,0:T(2,128)(2,1)S(1)} %get-tuple-element.24), channel_id=1, source_target_pairs={{0,16},{4,20},{8,24},{12,28},{16,32},{20,36},{24,40},{28,44},{32,4... | collective-permute-start | bytes 589832 | tf_op jit(solution)/shard_map/ppermute | solution.py:12
  76.5 34.1 %copy-start.2 = (bf16[1,64,10,6,128]{4,2,3,1,0:T(8,128)(2,1)}, bf16[1,64,10,6,128]{4,2,3,1,0:T(8,128)(2,1)S(1)}, u32[]{:S(2)}) copy-start(bf16[1,64,10,6,128]{4,2,3,1,0:T(8,128)(2,1)S(1)} %get-tuple-element.23) | copy-start | bytes 2949124
  87.5 2.3 copy-start.13
  101.2 3.7 copy-start.6
  106.6 0.8 copy-start.7
  108.0 50.1 %collective-permute-start.6 = (bf16[1,64,8,1,128]{4,2,3,1,0:T(8,128)(2,1)}, bf16[1,64,8,1,128]{4,2,3,1,0:T(8,128)(2,1)}, u32[]{:S(2)}, u32[]{:S(2)}) collective-permute-start(bf16[1,64,8,1,128]{4,2,3,1,0:T(8,128)(2,1)} %slice.94), channel_id=1, source_target_pairs={{0,4},{4,8},{8,12},{12,16},{16,20},{20,24},{24,28},{28,32},{32,36}... | collective-permute-start | bytes 393224 | tf_op jit(solution)/shard_map/ppermute | solution.py:12
  117.5 33.0 %copy-start.3 = (bf16[1,64,10,6,128]{4,2,3,1,0:T(8,128)(2,1)S(1)}, bf16[1,64,10,6,128]{4,2,3,1,0:T(8,128)(2,1)}, u32[]{:S(2)}) copy-start(bf16[1,64,10,6,128]{4,2,3,1,0:T(8,128)(2,1)} %copy-done.2) | copy-start | bytes 2949124
  157.7 1.0 copy-start.8
  157.7 6.6 %copy-start.14 = (pred[8,17]{0,1:T(8,128)(4,1)S(1)}, pred[8,17]{0,1:T(8,128)(4,1)}, u32[]{:S(2)}) copy-start(pred[8,17]{0,1:T(8,128)(4,1)} %constant.52) | copy-start | bytes 412
  158.9 10.2 %collective-permute-start.7 = (bf16[1,64,1,5,128]{4,2,3,1,0:T(2,128)(2,1)S(1)}, bf16[1,64,1,5,128]{4,2,3,1,0:T(2,128)(2,1)S(1)}, u32[]{:S(2)}, u32[]{:S(2)}) collective-permute-start(bf16[1,64,1,5,128]{4,2,3,1,0:T(2,128)(2,1)S(1)} %pad_maximum_fusion.8), channel_id=1, source_target_pairs={{0,16},{4,20},{8,24},{12,28},{16,32},{20,36},{24,40},{28,44},{32,4... | collective-permute-start | bytes 245768 | tf_op jit(solution)/shard_map/ppermute | solution.py:12
  169.6 5.8 %copy-start.12 = (bf16[1,1,4,2,64,128]{5,4,3,2,1,0:T(8,128)(2,1)S(1)}, bf16[1,1,4,2,64,128]{5,4,3,2,1,0:T(8,128)(2,1)}, u32[]{:S(2)}) copy-start(bf16[1,1,4,2,64,128]{5,4,3,2,1,0:T(8,128)(2,1)} %param.4) | copy-start | bytes 393220
  194.0 1.0 copy-start.11
  194.0 1.0 copy-start.15
  449.9 2.3 copy-start.10
Sparse Core Ops, SparseCore 0:
  184.0 265.8 all-reduce.2
where the time goes:
time: 469 us; the launch traced here: 460 us
  waiting for transfers between devices  274 us (58%)
  local copies, waits for them, and re-layouts  73.7 us (16%)
  matrix products  58.8 us (13%)
  starting transfers between devices  27.7 us (6%)
  between operations  15.1 us (3%)
  other arithmetic  10.8 us (2%)
    psum x1, waiting for transfers between devices, per_device(): conv_total = lax.psum(conv_local, ('slab', 'group'))  253 us
    transpose x1, matrix products, per_device(): conv_local = jnp.transpose(conv_local, (2, 3, 4, 0, 1))  33 us
    ppermute x8, starting transfers between devices, passed_along(): return lax.ppermute(block, axis, route)  27.7 us
    conv_general_dilated x22, local copies, waits for them, and re-layouts, convolve(): lax.conv_general_dilated(left, right, strides, padding, lhs_dilation=inpu...  23.6 us
    unnamed x42, local copies, waits for them, and re-layouts  23.1 us
    ppermute x8, waiting for transfers between devices, passed_along(): return lax.ppermute(block, axis, route)  21.1 us
    conv_general_dilated x4, matrix products, convolve(): lax.conv_general_dilated(left, right, strides, padding, lhs_dilation=inpu...  17.4 us
    slice x3, local copies, waits for them, and re-layouts, per_device(): padded = padded_pair[0:1]  9.38 us
  transfers between devices with their start and end apart: 9, of which 5 were waited for; matrix products, arithmetic and copies ran while one was open for 17% of the time, Pallas kernels for 0%

commit v1 on v0

v1 whole, which is shorter than its diff:
```python
import functools
import math

import jax
import jax.numpy as jnp
from jax import lax
from jax.experimental import pallas as pl
from jax.experimental.pallas import tpu as pltpu
from jax.sharding import PartitionSpec as P

MESH = pl.DeviceIdType.MESH
F32 = jnp.float32
BF16 = jnp.bfloat16
PY = 4
CIN = 128
C = 64
NT = (((1,), (1,)), ((), ()))

DIRS = [(0, 1), (0, -1), (1, 0), (-1, 0), (1, 1), (1, -1), (-1, 1), (-1, -1)]
COT_Z = {1: (6, 2), 0: (0, 8), -1: (0, 1)}
COT_Y = {1: (256, 256), 0: (0, 512), -1: (0, 128)}
COA_Z = {1: (3, 1), 0: (0, 4), -1: (0, 1)}
COA_Y = {1: (1, 1), 0: (0, 2), -1: (0, 1)}


def dot(a, b):
    return jnp.dot(a, b, preferred_element_type=F32)


def dot_nt(a, b):
    return lax.dot_general(a, b, NT, preferred_element_type=F32)


def ceil16(n):
    return -(-n // 16) * 16


class Place:
    def __init__(self, nz, ny, nx):
        self.nz, self.ny, self.nx = nz, ny, nx
        self.plane = ny * nx
        self.slab = lax.axis_index("slab")
        self.x = lax.axis_index("group")
        self.core = lax.rem(self.slab, 2)
        chip = lax.div(self.slab, 2)
        self.y = lax.rem(chip, ny)
        self.z = lax.div(chip, ny)
        self.p = self.y * nx + self.x
        lane = lax.rem(self.slab, PY)
        zb = lax.div(self.slab, PY)
        self.has_y = {1: lane < PY - 1, -1: lane > 0}
        self.has_z = {1: zb < nz * ny * 2 // PY - 1, -1: zb > 0}

    def has(self, dz, dy):
        if dz == 0:
            return self.has_y[dy]
        if dy == 0:
            return self.has_z[dz]
        return jnp.logical_and(self.has_z[dz], self.has_y[dy])

    def halo(self, dz, dy):
        return (self.slab + PY * dz + dy, self.x)

    def pair(self):
        return (self.slab + 1 - 2 * self.core, self.x)

    def in_plane(self, k):
        p = lax.rem(self.p + k, self.plane)
        y, x = lax.div(p, self.nx), lax.rem(p, self.nx)
        return p, ((self.z * self.ny + y) * 2 + self.core, x)

    def along_z(self, k):
        z = lax.rem(self.z + k, self.nz)
        return ((z * self.ny + self.y) * 2 + self.core, self.x)


def remote(src, dst, send, recv, device):
    return pltpu.make_async_remote_copy(
        src_ref=src, dst_ref=dst, send_sem=send, recv_sem=recv, device_id=device, device_id_type=MESH
    )


class Reduction:
    def __init__(self, at, rows, bufs, sems):
        self.at, self.r = at, rows
        self.v, self.r0, self.s0, self.r1, self.s1, self.r2, self.g = bufs
        self.pair_sems, self.plane_send, self.plane_recv, self.z_send, self.z_recv, self.back_send, self.back_recv = sems
        self.sent = []

    def go(self, copy):
        copy.start()
        self.sent.append(copy)
        return copy

    def start_pair(self):
        at = self.at
        self.c0 = self.go(remote(self.v.at[1 - at.core], self.r0, self.pair_sems.at[0], self.pair_sems.at[1], at.pair()))

    def start_plane(self):
        at, r = self.at, self.r
        self.c0.wait_recv()
        self.s0[...] = (self.v[at.core].astype(F32) + self.r0[...].astype(F32)).astype(BF16)
        self.c1 = []
        for k in range(1, at.plane):
            p, device = at.in_plane(k)
            rows = pl.ds(pl.multiple_of(p * r, 16), r)
            self.c1.append(
                self.go(remote(self.s0.at[rows], self.r1.at[k - 1], self.plane_send.at[k - 1], self.plane_recv.at[k - 1], device))
            )

    def start_z(self):
        at, r = self.at, self.r
        total = self.s0[pl.ds(pl.multiple_of(at.p * r, 16), r), :].astype(F32)
        for k, c in enumerate(self.c1):
            c.wait_recv()
            total = total + self.r1[k].astype(F32)
        self.s1[...] = total.astype(BF16)
        self.r2[at.z] = self.s1[...]
        self.c2 = []
        for k in range(1, at.nz):
            self.c2.append(
                self.go(remote(self.s1, self.r2.at[at.z], self.z_send.at[k - 1], self.z_recv.at[k - 1], at.along_z(k)))
            )

    def start_back(self):
        at, r = self.at, self.r
        for c in self.c2:
            c.wait_recv()
        total = self.r2[0].astype(F32)
        for k in range(1, at.nz):
            total = total + self.r2[k].astype(F32)
        rows = pl.ds(pl.multiple_of(at.p * r, 16), r)
        self.g[at.core, rows, :] = total.astype(BF16)
        self.c3 = []
        for k in range(1, at.plane):
            _, device = at.in_plane(k)
            self.c3.append(
                self.go(
                    remote(
                        self.g.at[at.core, rows], self.g.at[at.core, rows], self.back_send.at[k - 1], self.back_recv.at[k - 1], device
                    )
                )
            )

    def start_share(self):
        at = self.at
        for c in self.c3:
            c.wait_recv()
        self.c4 = self.go(
            remote(self.g.at[at.core], self.g.at[at.core], self.pair_sems.at[2], self.pair_sems.at[3], at.pair())
        )

    def finish(self):
        self.c4.wait_recv()
        for c in self.sent:
            c.wait_send()


def kernel(
    dims,
    rows_of,
    coarse_hbm,
    tw_hbm,
    cw_hbm,
    cot_hbm,
    field_out,
    gc_out,
    gcw_out,
    gtw_out,
    coarse,
    tw,
    cw,
    cot,
    wide,
    rows_cot,
    *rest,
):
    rest = list(rest)
    cot_halo = {d: rest.pop(0) for d in DIRS}
    coa_halo = {d: rest.pop(0) for d in DIRS}
    up, w1, w2, w4, w3, act, ds, bb, gh, taps, et, cols, pair_buf = (rest.pop(0) for _ in range(13))
    bufs = [[rest.pop(0) for _ in range(7)] for _ in range(2)]
    sems = [[rest.pop(0) for _ in range(7)] for _ in range(2)]
    load_sem, cot_send, cot_recv, coa_send, coa_recv = rest
    nz, ny, nx = dims
    at = Place(nz, ny, nx)

    barrier = pltpu.get_barrier_semaphore()
    others = [at.pair()]
    others += [at.in_plane(k)[1] for k in range(1, at.plane)]
    others += [at.along_z(k) for k in range(1, nz)]
    for device in others:
        pl.semaphore_signal(barrier, inc=1, device_id=device, device_id_type=MESH)
    for d in DIRS:

        @pl.when(at.has(*d))
        def _():
            pl.semaphore_signal(barrier, inc=1, device_id=at.halo(*d), device_id_type=MESH)

    loads = [
        pltpu.make_async_copy(src, dst, load_sem.at[i])
        for i, (src, dst) in enumerate(((cot_hbm, cot), (coarse_hbm, coarse), (tw_hbm, tw), (cw_hbm, cw)))
    ]
    for load in loads:
        load.start()

    loads[0].wait()
    wide[...] = cot[...].astype(F32)
    for z in range(8):
        for y in range(4):
            rows_cot[z, :, y * 128 : y * 128 + 128] = wide[pl.ds(z * 4 + y, C, stride=32), :].astype(BF16)

    for d in DIRS:

        @pl.when(jnp.logical_not(at.has(-d[0], -d[1])))
        def _():
            cot_halo[d][...] = jnp.zeros_like(cot_halo[d])
            coa_halo[d][...] = jnp.zeros_like(coa_halo[d])

    loads[1].wait()
    count = len(others)
    for d in DIRS:
        count = count + jnp.where(at.has(*d), 1, 0)
    pl.semaphore_wait(barrier, count)

    def coa_copy(i, d):
        (z, dz), (y, dy) = COA_Z[d[0]], COA_Y[d[1]]
        return remote(
            coarse.at[pl.ds(z, dz), pl.ds(y, dy)], coa_halo[d], coa_send.at[i], coa_recv.at[i], at.halo(*d)
        )

    def cot_copy(i, d):
        (z, dz), (y, dy) = COT_Z[d[0]], COT_Y[d[1]]
        return remote(
            rows_cot.at[pl.ds(z, dz), :, pl.ds(y, dy)], cot_halo[d], cot_send.at[i], cot_recv.at[i], at.halo(*d)
        )

    for copy_of in (coa_copy, cot_copy):
        for i, d in enumerate(DIRS):

            @pl.when(at.has(*d))
            def _():
                copy_of(i, d).start()

    def arrived(copy_of):
        for i, d in enumerate(DIRS):

            @pl.when(at.has(-d[0], -d[1]))
            def _():
                copy_of(i, d).wait_recv()

    loads[2].wait()
    loads[3].wait()
    for kz in range(3):
        for ky in range(3):
            for kx in range(3):
                block = tw[((kz * 3 + ky) * 3 + kx) * C : ((kz * 3 + ky) * 3 + kx + 1) * C, :]
                w1[kz, ky * C : (ky + 1) * C, kx * 128 : kx * 128 + 128] = block
                w3[ky * 3 + kx, kz * C : (kz + 1) * C, :] = block
    for a in range(3):
        tall = jnp.concatenate([cw[(b * 3 + a) * 192 : (b * 3 + a + 1) * 192, :].astype(F32) for b in range(3)], axis=0)
        w4[a * C : (a + 1) * C, :] = tall.T.astype(BF16)
        w2[a * C : (a + 1) * C, :] = jnp.concatenate(
            [
                cw[((b * 3 + a) * 3 + x) * C : ((b * 3 + a) * 3 + x + 1) * C, :].astype(F32)
                for b in (2, 1, 0)
                for x in range(3)
            ],
            axis=1,
        ).astype(BF16)

    lane_at = lax.broadcasted_iota(jnp.int32, (C, 128), 1)
    not_first = jnp.where(lane_at == 0, 0.0, 1.0).astype(F32)
    not_last = jnp.where(lane_at == 127, 0.0, 1.0).astype(F32)

    def taps_of(row):
        return pltpu.roll(row, 1, 1) * not_first, row, pltpu.roll(row, 127, 1) * not_last

    def put_cot(ze, ye, row):
        before, row, after = taps_of(row.astype(F32))
        for i, value in enumerate((after, row, before)):
            bb[pl.ds(pl.multiple_of(ze * 192 + i * C, C), C), ye * 128 : ye * 128 + 128] = value.astype(BF16)

    @pl.loop(0, 8)
    def _(z):
        for y in range(4):
            put_cot(z + 2, y + 2, rows_cot[z, :, y * 128 : y * 128 + 128])

    cell = lax.broadcasted_iota(jnp.int32, (C, 384), 0)
    place = lax.broadcasted_iota(jnp.int32, (C, 384), 1)
    spread = jnp.zeros((C, 384), F32)
    for k in range(3):
        spread = spread + jnp.where(place == 2 * cell + (k - 1) + 128 * k, 1.0, 0.0) * jnp.where(
            jnp.logical_and(place >= 128 * k, place < 128 * k + 128), 1.0, 0.0
        )
    spread = spread.astype(BF16)

    def put_coarse(ze, ye, block):
        wide_block = dot(block.astype(F32).T.astype(BF16), spread).astype(BF16)
        for k in range(3):
            up[pl.ds(pl.multiple_of(ze * 384 + k * 128, 128), 128), ye * 128 : ye * 128 + 128] = wide_block[:, k * 128 : k * 128 + 128]

    @pl.loop(0, 4)
    def _(z):
        for y in range(2):
            put_coarse(z + 1, y + 1, coarse[z, y])

    arrived(coa_copy)

    @pl.loop(0, 4)
    def _(z):
        put_coarse(z + 1, 0, coa_halo[(0, 1)][z, 0])
        put_coarse(z + 1, 3, coa_halo[(0, -1)][z, 0])

    for dz, ze in ((1, 0), (-1, 5)):
        put_coarse(ze, 0, coa_halo[(dz, 1)][0, 0])
        for y in range(2):
            put_coarse(ze, y + 1, coa_halo[(dz, 0)][0, y])
        put_coarse(ze, 3, coa_halo[(dz, -1)][0, 0])

    has_zl = jnp.where(at.has_z[-1], 1.0, 0.0).astype(F32)
    has_zh = jnp.where(at.has_z[1], 1.0, 0.0).astype(F32)
    has_yl = jnp.where(at.has_y[-1], 1.0, 0.0).astype(F32)
    has_yh = jnp.where(at.has_y[1], 1.0, 0.0).astype(F32)

    def put_hidden(zf, partial, z_mask, slopes):
        for yf in range(6):
            n = yf // 2
            if yf % 2:
                h = partial[C : 2 * C, (n + 1) * 128 : (n + 2) * 128]
            else:
                h = partial[2 * C :, n * 128 : n * 128 + 128] + partial[:C, (n + 1) * 128 : (n + 2) * 128]
            mask = z_mask
            if yf == 0:
                mask = mask * has_yl
            if yf == 5:
                mask = mask * has_yh
            s = 1.0 / (1.0 + jnp.exp(-h))
            row = (h * s) * mask
            for i, value in enumerate(taps_of(row)):
                act[pl.ds(pl.multiple_of(zf * 192 + i * C, C), C), yf * 128 : yf * 128 + 128] = value.astype(BF16)
            if yf < 5:

                @pl.when(slopes)
                def _():
                    ds[zf, :, yf * 128 : yf * 128 + 128] = s * (1.0 + h * (1.0 - s)) * (mask if yf == 0 else z_mask)

    w1_odd = jnp.concatenate([w1[2], w1[0]], axis=1)

    @pl.loop(0, 5)
    def _(m):
        start = pl.multiple_of(m * 384, 128)
        odd = dot(w1_odd, up[pl.ds(start, 768), :])
        put_hidden(2 * m, odd, jnp.where(m == 0, has_zl, 1.0), m >= 0)
        even = dot(w1[1], up[pl.ds(pl.multiple_of(start + 384, 128), 384), :])
        put_hidden(2 * m + 1, even, jnp.where(m == 4, has_zh, 1.0), m < 4)

    gc_v, gt_v = bufs[0][0], bufs[1][0]
    conv_sum = Reduction(at, rows_of[0], bufs[0], sems[0])
    tconv_sum = Reduction(at, rows_of[1], bufs[1], sems[1])
    taps[...] = jnp.zeros_like(taps)

    @pl.loop(0, 8)
    def _(z):
        blocks = [
            act[pl.ds(pl.multiple_of((z + dz) * 192 + C, C), C), dy * 128 : dy * 128 + 512]
            for dz in range(3)
            for dy in range(3)
        ]
        right = bb[pl.ds(pl.multiple_of((z + 2) * 192, C), 192), 256:768]
        taps[...] += dot_nt(jnp.concatenate(blocks, axis=0), right)

    def fill(v, half_rows, parts):
        at_row = 0
        for part in parts:
            done, n = 0, part.shape[0]
            while done < n:
                half, row = divmod(at_row, half_rows)
                m = min(n - done, half_rows - row)
                v[half, row : row + m, :] = part[done : done + m, :].astype(BF16)
                done, at_row = done + m, at_row + m
        while at_row < 2 * half_rows:
            half, row = divmod(at_row, half_rows)
            v[half, row:, :] = jnp.zeros((half_rows - row, 128), BF16)
            at_row += half_rows - row

    fill(
        gc_v,
        at.plane * rows_of[0],
        [taps[:, :128], jnp.concatenate([taps[:288, 128:], taps[288:, 128:]], axis=1)],
    )
    conv_sum.start_pair()

    arrived(cot_copy)

    @pl.loop(0, 8)
    def _(z):
        for y in range(2):
            put_cot(z + 2, y, cot_halo[(0, 1)][z, :, y * 128 : y * 128 + 128])
        put_cot(z + 2, 6, cot_halo[(0, -1)][z])

    for dz, planes in ((1, 2), (-1, 1)):
        for z in range(planes):
            ze = z if dz > 0 else 10
            for y in range(2):
                put_cot(ze, y, cot_halo[(dz, 1)][z, :, y * 128 : y * 128 + 128])
            for y in range(4):
                put_cot(ze, y + 2, cot_halo[(dz, 0)][z, :, y * 128 : y * 128 + 128])
            put_cot(ze, 6, cot_halo[(dz, -1)][z])
    conv_sum.start_plane()

    @pl.loop(0, 9)
    def _(q):
        partial = dot(w2[...], bb[pl.ds(pl.multiple_of(q * 192, C), 576), :])
        for yf in range(5):
            ga = partial[:C, (yf + 2) * 128 : (yf + 3) * 128]
            ga = ga + partial[C : 2 * C, (yf + 1) * 128 : (yf + 2) * 128]
            ga = ga + partial[2 * C :, yf * 128 : yf * 128 + 128]
            gh[pl.ds(pl.multiple_of(q * C, C), C), yf * 128 : yf * 128 + 128] = (
                ga * ds[q, :, yf * 128 : yf * 128 + 128]
            ).astype(BF16)

    conv_sum.start_z()

    def picks(shape, f_dim):
        f = lax.broadcasted_iota(jnp.int32, shape, f_dim)
        c = lax.broadcasted_iota(jnp.int32, shape, 1 - f_dim)
        out = jnp.zeros(shape, F32)
        for k in range(3):
            for y in range(2):
                cell0 = k * 128 + y * C
                inside = jnp.logical_and(c >= cell0, c < cell0 + C)
                hit = jnp.logical_and(f == 2 * (c - cell0) + (k - 1) + 128 * y, inside)
                own = jnp.logical_and(f >= 128 * y, f < 128 * y + 128)
                out = out + jnp.where(jnp.logical_and(hit, own), 1.0, 0.0)
        return out.astype(BF16)

    pick = picks((256, 384), 0)
    pick_t = picks((384, 256), 1)
    for ky in range(3):
        pair_buf[:, :128] = gh[:, ky * 128 : ky * 128 + 128]
        pair_buf[:, 128:] = gh[:, (ky + 2) * 128 : (ky + 3) * 128]
        some = dot(pair_buf[...], pick).astype(BF16)
        for zc in range(4):
            for kz in range(3):
                for kx in range(3):
                    row = ((kz * 3 + ky) * 3 + kx) * C
                    q = (2 * zc + kz) * C
                    cols[row : row + C, zc * 128 : zc * 128 + 128] = some[q : q + C, kx * 128 : kx * 128 + 128]
        et[ky] = dot_nt(pick_t, pair_buf[...]).astype(BF16)

    fill(gt_v, at.plane * rows_of[1], [dot(cols[...], coarse[...].reshape(512, CIN))])
    tconv_sum.start_pair()
    conv_sum.start_back()

    for zc in range(4):
        total = jnp.zeros((128, CIN), F32)
        for ky in range(3):
            for kx in range(3):
                total = total + dot(et[ky, kx * 128 : kx * 128 + 128, zc * 128 : zc * 128 + 192], w3[ky * 3 + kx])
        gc_out[zc * 128 : zc * 128 + 128, :] = total.astype(BF16)
    tconv_sum.start_plane()

    def put_field(z):
        partial = dot(w4[...], act[pl.ds(pl.multiple_of(z * 192, C), 576), :])
        for y in range(4):
            row = partial[:C, y * 128 : y * 128 + 128]
            row = row + partial[C : 2 * C, (y + 1) * 128 : (y + 2) * 128]
            row = row + partial[2 * C :, (y + 2) * 128 : (y + 3) * 128]
            wide[pl.ds(z * 4 + y, C, stride=32), :] = row

    pl.loop(0, 4)(put_field)
    conv_sum.start_share()
    tconv_sum.start_z()
    pl.loop(4, 8)(put_field)
    tconv_sum.start_back()
    field_out[...] = wide[...].astype(BF16)

    n_dev = nz * ny * nx * 2
    conv_sum.finish()
    conv_scale = 1.0 / math.sqrt(n_dev * 8 * 4 * 128)
    g = conv_sum.g[...].reshape(-1, 128)
    first = g[:576].astype(F32) * conv_scale
    second = g[576:864].astype(F32) * conv_scale
    for zy in range(9):
        for dx in range(2):
            gcw_out[zy * 3 + dx] = first[zy * C : (zy + 1) * C, dx * C : (dx + 1) * C]
    for half in range(18):
        src = second[(half % 9) * 32 : (half % 9) * 32 + 32, (half // 9) * C : (half // 9 + 1) * C]
        gcw_out[(half // 2) * 3 + 2, (half % 2) * 32 : (half % 2) * 32 + 32, :] = src
    tconv_sum.start_share()
    tconv_sum.finish()
    tconv_scale = 1.0 / math.sqrt(n_dev * 4 * 2 * 64)
    gtw_out[...] = tconv_sum.g[...].reshape(-1, 128)[:1728].astype(F32) * tconv_scale

    for copy_of in (coa_copy, cot_copy):
        for i, d in enumerate(DIRS):

            @pl.when(at.has(*d))
            def _():
                copy_of(i, d).wait_send()


def solution(mesh):
    nx = mesh.shape["group"]
    n_slab = mesh.shape["slab"]
    ny = 4
    nz = n_slab // (2 * ny)
    plane = ny * nx
    rows_of = [ceil16(-(-n // (2 * plane))) for n in (864, 1728)]

    def step(coarse, tw, cw, cot):
        dma = pltpu.SemaphoreType.DMA
        vmem = pltpu.VMEM
        scratch = [
            vmem((4, 2, 64, CIN), BF16),
            vmem((27 * C, CIN), BF16),
            vmem((27 * C, C), BF16),
            vmem((2048, 128), BF16),
            vmem((2048, 128), F32),
            vmem((8, C, 512), BF16),
        ]
        scratch += [vmem((COT_Z[dz][1], C, COT_Y[dy][1]), BF16) for dz, dy in DIRS]
        scratch += [vmem((COA_Z[dz][1], COA_Y[dy][1], 64, CIN), BF16) for dz, dy in DIRS]
        scratch += [
            vmem((6 * 384, 512), BF16),
            vmem((3, 192, 384), BF16),
            vmem((192, 576), BF16),
            vmem((192, 576), BF16),
            vmem((9, 192, CIN), BF16),
            vmem((10 * 192, 768), BF16),
            vmem((9, C, 640), F32),
            vmem((11 * 192, 896), BF16),
            vmem((9 * C, 640), BF16),
            vmem((576, 192), F32),
            vmem((3, 384, 576), BF16),
            vmem((1728, 512), BF16),
            vmem((576, 256), BF16),
        ]
        for r in rows_of:
            scratch += [
                vmem((2, plane * r, 128), BF16),
                vmem((plane * r, 128), BF16),
                vmem((plane * r, 128), BF16),
                vmem((plane - 1, r, 128), BF16),
                vmem((r, 128), BF16),
                vmem((nz, r, 128), BF16),
                vmem((2, plane * r, 128), BF16),
            ]
        for r in rows_of:
            scratch += [dma((4,)), dma((plane - 1,)), dma((plane - 1,)), dma((nz - 1,)), dma((nz - 1,))]
            scratch += [dma((plane - 1,)), dma((plane - 1,))]
        scratch += [dma((4,)), dma((8,)), dma((8,)), dma((8,)), dma((8,))]
        any_space = pl.BlockSpec(memory_space=pl.ANY)
        in_vmem = pl.BlockSpec(memory_space=pltpu.VMEM)
        field, gc, gcw, gtw = pl.pallas_call(
            functools.partial(kernel, (nz, ny, nx), rows_of),
            out_shape=(
                jax.ShapeDtypeStruct((2048, 128), BF16),
                jax.ShapeDtypeStruct((512, CIN), BF16),
                jax.ShapeDtypeStruct((27, C, C), F32),
                jax.ShapeDtypeStruct((27 * C, CIN), F32),
            ),
            in_specs=[any_space] * 4,
            out_specs=(in_vmem,) * 4,
            scratch_shapes=scratch,
            compiler_params=pltpu.CompilerParams(
                collective_id=0, has_side_effects=True, vmem_limit_bytes=50 * 2**20
            ),
            cost_estimate=pl.CostEstimate(flops=7 * 10**9, bytes_accessed=4 * 10**6, transcendentals=500000),
        )(
            coarse.reshape(4, 2, 64, CIN),
            jnp.swapaxes(tw, 3, 4).reshape(27 * C, CIN),
            cw.reshape(27 * C, C),
            cot.reshape(2048, 128),
        )
        return (
            field.reshape(1, 1, C, 8, 4, 128),
            gc.reshape(1, 1, 4, 2, 64, CIN),
            gcw.reshape(3, 3, 3, C, C),
            jnp.swapaxes(gtw.reshape(3, 3, 3, C, CIN), 3, 4),
        )

    blocks = P("group", "slab", None, None, None, None)
    return jax.shard_map(
        step,
        mesh=mesh,
        in_specs=(blocks, P(), P(), blocks),
        out_specs=(blocks, blocks, P(), P()),
        check_vma=False,
    )
```

time: 469 us -> 73.8 us (0.16)
  the two profiles are of different devices: /device:TPU:2 before, /device:TPU:1 now
where the time goes in v1:
time: 73.8 us; the launch traced here: 73.5 us
  Pallas kernels  65.6 us (89%)
  local copies, waits for them, and re-layouts  7.24 us (10%)
    pallas_call x1, Pallas kernels, step(): pl.pallas_call(functools.partial(kernel, (nz, ny, nx), rows_of), out_shap...  65.6 us
    unnamed x12, local copies, waits for them, and re-layouts  7.24 us

profile of v1, /device:TPU:1, one launch (start us, length us, event | category | flops | bytes accessed | tf_op | source)
XLA Modules:
  0.0 73.5 jit_solution(5370538609929263539)
XLA Ops:
  0.6 0.0 copy-start
  0.6 1.0 %copy-done = bf16[1,1,64,8,4,128]{5,4,3,2,1,0:T(4,128)(2,1)S(1)} copy-done((bf16[1,1,64,8,4,128]{5,4,3,2,1,0:T(4,128)(2,1)S(1)}, bf16[1,1,64,8,4,128]{5,4,3,2,1,0:T(4,128)(2,1)}, u32[]{:S(2)}) %copy-start) | copy-done | bytes 524312
  1.7 0.0 copy-start.1
  1.7 1.0 %copy-done.1 = bf16[3,3,3,128,64]{3,4,2,1,0:T(8,128)(2,1)S(1)} copy-done((bf16[3,3,3,128,64]{3,4,2,1,0:T(8,128)(2,1)S(1)}, bf16[3,3,3,128,64]{3,4,2,1,0:T(8,128)(2,1)}, u32[]{:S(2)}) %copy-start.1) | copy-done | bytes 442392
  2.7 0.0 copy-start.2
  2.7 1.0 %copy-done.2 = bf16[3,3,3,64,64]{4,3,2,1,0:T(8,128)(2,1)S(1)} copy-done((bf16[3,3,3,64,64]{4,3,2,1,0:T(8,128)(2,1)S(1)}, bf16[3,3,3,64,64]{4,3,2,1,0:T(8,128)(2,1)}, u32[]{:S(2)}) %copy-start.2) | copy-done | bytes 221208
  3.7 0.0 copy-start.3
  3.7 0.9 %copy-done.3 = bf16[1,1,4,2,64,128]{5,4,3,2,1,0:T(8,128)(2,1)S(1)} copy-done((bf16[1,1,4,2,64,128]{5,4,3,2,1,0:T(8,128)(2,1)S(1)}, bf16[1,1,4,2,64,128]{5,4,3,2,1,0:T(8,128)(2,1)}, u32[]{:S(2)}) %copy-start.3) | copy-done | bytes 131096
  4.6 65.6 %shard_map.75 = (bf16[2048,128]{1,0:T(8,128)(2,1)S(1)}, bf16[512,128]{1,0:T(8,128)(2,1)S(1)}, f32[27,64,64]{2,1,0:T(8,128)S(1)}, f32[1728,128]{1,0:T(8,128)S(1)}) custom-call(bf16[4,2,64,128]{3,2,1,0:T(8,128)(2,1)S(1)} %bitcast.19, bf16[1728,128]{1,0:T(8,128)(2,1)S(1)} %bitcast.17, bf16[1728,64]{1,0:T(8,128)(2,1)S(1)} %bitcast.18, bf16[2048,128]{1,0:T(8,128)(2,1)S(1)} %bitcast.16), custom_call_target="tpu_custom_call" | custom-call | flops 7000000000 | bytes 4000000 | tf_op jit(solution)/shard_map/pallas_call | solution.py:556
  70.2 0.8 %copy.12 = bf16[1,1,64,8,4,128]{5,4,3,2,1,0:T(4,128)(2,1)} copy(bf16[1,1,64,8,4,128]{5,4,3,2,1,0:T(4,128)(2,1)S(1)} %bitcast.14) | data formatting | bytes 1048576
  71.0 0.7 copy.13
  71.7 0.9 %copy.14 = f32[3,3,3,64,64]{4,3,2,1,0:T(8,128)} copy(f32[3,3,3,64,64]{4,3,2,1,0:T(8,128)S(1)} %bitcast.13) | data formatting | bytes 884736
  72.6 0.9 %copy.15 = f32[3,3,3,128,64]{3,4,2,1,0:T(8,128)} copy(f32[3,3,3,128,64]{3,4,2,1,0:T(8,128)S(1)} %bitcast.12) | data formatting | bytes 1769472
Async XLA Ops:
  0.6 1.0 %copy-start = (bf16[1,1,64,8,4,128]{5,4,3,2,1,0:T(4,128)(2,1)S(1)}, bf16[1,1,64,8,4,128]{5,4,3,2,1,0:T(4,128)(2,1)}, u32[]{:S(2)}) copy-start(bf16[1,1,64,8,4,128]{5,4,3,2,1,0:T(4,128)(2,1)} %param.7) | copy-start | bytes 1572868
  1.7 1.0 %copy-start.1 = (bf16[3,3,3,128,64]{3,4,2,1,0:T(8,128)(2,1)S(1)}, bf16[3,3,3,128,64]{3,4,2,1,0:T(8,128)(2,1)}, u32[]{:S(2)}) copy-start(bf16[3,3,3,128,64]{3,4,2,1,0:T(8,128)(2,1)} %param.5) | copy-start | bytes 1327108
  2.7 1.0 %copy-start.2 = (bf16[3,3,3,64,64]{4,3,2,1,0:T(8,128)(2,1)S(1)}, bf16[3,3,3,64,64]{4,3,2,1,0:T(8,128)(2,1)}, u32[]{:S(2)}) copy-start(bf16[3,3,3,64,64]{4,3,2,1,0:T(8,128)(2,1)} %param.6) | copy-start | bytes 663556
  3.7 0.9 %copy-start.3 = (bf16[1,1,4,2,64,128]{5,4,3,2,1,0:T(8,128)(2,1)S(1)}, bf16[1,1,4,2,64,128]{5,4,3,2,1,0:T(8,128)(2,1)}, u32[]{:S(2)}) copy-start(bf16[1,1,4,2,64,128]{5,4,3,2,1,0:T(8,128)(2,1)} %param.4) | copy-start | bytes 393220

commit v2 on v1

--- a/solution.py
+++ b/solution.py
@@ -29,6 +29,18 @@
 
 def dot_nt(a, b):
     return lax.dot_general(a, b, NT, preferred_element_type=F32)
+
+
+def mult(n, of):
+    return n
+
+
+def unrolled(start, stop):
+    def run(body):
+        for i in range(start, stop):
+            body(i)
+
+    return run
 
 
 def ceil16(n):
@@ -279,9 +291,9 @@
     def put_cot(ze, ye, row):
         before, row, after = taps_of(row.astype(F32))
         for i, value in enumerate((after, row, before)):
-            bb[pl.ds(pl.multiple_of(ze * 192 + i * C, C), C), ye * 128 : ye * 128 + 128] = value.astype(BF16)
-
-    @pl.loop(0, 8)
+            bb[pl.ds(mult(ze * 192 + i * C, C), C), ye * 128 : ye * 128 + 128] = value.astype(BF16)
+
+    @unrolled(0, 8)
     def _(z):
         for y in range(4):
             put_cot(z + 2, y + 2, rows_cot[z, :, y * 128 : y * 128 + 128])
@@ -298,16 +310,16 @@
     def put_coarse(ze, ye, block):
         wide_block = dot(block.astype(F32).T.astype(BF16), spread).astype(BF16)
         for k in range(3):
-            up[pl.ds(pl.multiple_of(ze * 384 + k * 128, 128), 128), ye * 128 : ye * 128 + 128] = wide_block[:, k * 128 : k * 128 + 128]
-
-    @pl.loop(0, 4)
+            up[pl.ds(mult(ze * 384 + k * 128, 128), 128), ye * 128 : ye * 128 + 128] = wide_block[:, k * 128 : k * 128 + 128]
+
+    @unrolled(0, 4)
     def _(z):
         for y in range(2):
             put_coarse(z + 1, y + 1, coarse[z, y])
 
     arrived(coa_copy)
 
-    @pl.loop(0, 4)
+    @unrolled(0, 4)
     def _(z):
         put_coarse(z + 1, 0, coa_halo[(0, 1)][z, 0])
         put_coarse(z + 1, 3, coa_halo[(0, -1)][z, 0])
@@ -331,43 +343,42 @@
             else:
                 h = partial[2 * C :, n * 128 : n * 128 + 128] + partial[:C, (n + 1) * 128 : (n + 2) * 128]
             mask = z_mask
-            if yf == 0:
-                mask = mask * has_yl
-            if yf == 5:
-                mask = mask * has_yh
-            s = 1.0 / (1.0 + jnp.exp(-h))
-            row = (h * s) * mask
+            if yf in (0, 5):
+                y_mask = has_yl if yf == 0 else has_yh
+                mask = y_mask if mask is None else mask * y_mask
+            s = 0.5 * jnp.tanh(0.5 * h) + 0.5
+            row = h * s
+            if mask is not None:
+                row = row * mask
             for i, value in enumerate(taps_of(row)):
-                act[pl.ds(pl.multiple_of(zf * 192 + i * C, C), C), yf * 128 : yf * 128 + 128] = value.astype(BF16)
-            if yf < 5:
-
-                @pl.when(slopes)
-                def _():
-                    ds[zf, :, yf * 128 : yf * 128 + 128] = s * (1.0 + h * (1.0 - s)) * (mask if yf == 0 else z_mask)
+                act[pl.ds(mult(zf * 192 + i * C, C), C), yf * 128 : yf * 128 + 128] = value.astype(BF16)
+            if yf < 5 and slopes:
+                slope = s * (1.0 + h * (1.0 - s))
+                ds[zf, :, yf * 128 : yf * 128 + 128] = slope if mask is None else slope * mask
 
     w1_odd = jnp.concatenate([w1[2], w1[0]], axis=1)
 
-    @pl.loop(0, 5)
+    @unrolled(0, 5)
     def _(m):
-        start = pl.multiple_of(m * 384, 128)
+        start = mult(m * 384, 128)
         odd = dot(w1_odd, up[pl.ds(start, 768), :])
-        put_hidden(2 * m, odd, jnp.where(m == 0, has_zl, 1.0), m >= 0)
-        even = dot(w1[1], up[pl.ds(pl.multiple_of(start + 384, 128), 384), :])
-        put_hidden(2 * m + 1, even, jnp.where(m == 4, has_zh, 1.0), m < 4)
+        put_hidden(2 * m, odd, has_zl if m == 0 else None, True)
+        even = dot(w1[1], up[pl.ds(mult(start + 384, 128), 384), :])
+        put_hidden(2 * m + 1, even, has_zh if m == 4 else None, m < 4)
 
     gc_v, gt_v = bufs[0][0], bufs[1][0]
     conv_sum = Reduction(at, rows_of[0], bufs[0], sems[0])
     tconv_sum = Reduction(at, rows_of[1], bufs[1], sems[1])
     taps[...] = jnp.zeros_like(taps)
 
-    @pl.loop(0, 8)
+    @unrolled(0, 8)
     def _(z):
         blocks = [
-            act[pl.ds(pl.multiple_of((z + dz) * 192 + C, C), C), dy * 128 : dy * 128 + 512]
+            act[pl.ds(mult((z + dz) * 192 + C, C), C), dy * 128 : dy * 128 + 512]
             for dz in range(3)
             for dy in range(3)
         ]
-        right = bb[pl.ds(pl.multiple_of((z + 2) * 192, C), 192), 256:768]
+        right = bb[pl.ds(mult((z + 2) * 192, C), 192), 256:768]
         taps[...] += dot_nt(jnp.concatenate(blocks, axis=0), right)
 
     def fill(v, half_rows, parts):
@@ -393,7 +404,7 @@
 
     arrived(cot_copy)
 
-    @pl.loop(0, 8)
+    @unrolled(0, 8)
     def _(z):
         for y in range(2):
             put_cot(z + 2, y, cot_halo[(0, 1)][z, :, y * 128 : y * 128 + 128])
@@ -409,14 +420,14 @@
             put_cot(ze, 6, cot_halo[(dz, -1)][z])
     conv_sum.start_plane()
 
-    @pl.loop(0, 9)
+    @unrolled(0, 9)
     def _(q):
-        partial = dot(w2[...], bb[pl.ds(pl.multiple_of(q * 192, C), 576), :])
+        partial = dot(w2[...], bb[pl.ds(mult(q * 192, C), 576), :])
         for yf in range(5):
             ga = partial[:C, (yf + 2) * 128 : (yf + 3) * 128]
             ga = ga + partial[C : 2 * C, (yf + 1) * 128 : (yf + 2) * 128]
             ga = ga + partial[2 * C :, yf * 128 : yf * 128 + 128]
-            gh[pl.ds(pl.multiple_of(q * C, C), C), yf * 128 : yf * 128 + 128] = (
+            gh[pl.ds(mult(q * C, C), C), yf * 128 : yf * 128 + 128] = (
                 ga * ds[q, :, yf * 128 : yf * 128 + 128]
             ).astype(BF16)
 
@@ -462,17 +473,17 @@
     tconv_sum.start_plane()
 
     def put_field(z):
-        partial = dot(w4[...], act[pl.ds(pl.multiple_of(z * 192, C), 576), :])
+        partial = dot(w4[...], act[pl.ds(mult(z * 192, C), 576), :])
         for y in range(4):
             row = partial[:C, y * 128 : y * 128 + 128]
             row = row + partial[C : 2 * C, (y + 1) * 128 : (y + 2) * 128]
             row = row + partial[2 * C :, (y + 2) * 128 : (y + 3) * 128]
             wide[pl.ds(z * 4 + y, C, stride=32), :] = row
 
-    pl.loop(0, 4)(put_field)
+    unrolled(0, 4)(put_field)
     conv_sum.start_share()
     tconv_sum.start_z()
-    pl.loop(4, 8)(put_field)
+    unrolled(4, 8)(put_field)
     tconv_sum.start_back()
     field_out[...] = wide[...].astype(BF16)
 

time: 73.8 us -> 64.3 us (0.87)
  Pallas kernels: 65.6 us -> 56.2 us
    pallas_call x1, Pallas kernels: 65.6 us -> 56.2 us  [step(): pl.pallas_call(functools.partial(kernel, (nz, ny, nx), rows_of), out_shap...]
where the time goes in v2:
time: 64.3 us; the launch traced here: 64 us
  Pallas kernels  56.2 us (87%)
  local copies, waits for them, and re-layouts  7.24 us (11%)
  between operations  0.65 us (1%)
    pallas_call x1, Pallas kernels, step(): pl.pallas_call(functools.partial(kernel, (nz, ny, nx), rows_of), out_shap...  56.2 us
    unnamed x12, local copies, waits for them, and re-layouts  7.24 us

profile of v2, /device:TPU:1, one launch (start us, length us, event | category | flops | bytes accessed | tf_op | source)
XLA Modules:
  0.0 64.0 jit_solution(3139550171961266531)
XLA Ops:
  0.6 0.0 copy-start
  0.6 1.0 %copy-done = bf16[1,1,64,8,4,128]{5,4,3,2,1,0:T(4,128)(2,1)S(1)} copy-done((bf16[1,1,64,8,4,128]{5,4,3,2,1,0:T(4,128)(2,1)S(1)}, bf16[1,1,64,8,4,128]{5,4,3,2,1,0:T(4,128)(2,1)}, u32[]{:S(2)}) %copy-start) | copy-done | bytes 524312
  1.7 0.0 copy-start.1
  1.7 1.0 %copy-done.1 = bf16[3,3,3,128,64]{3,4,2,1,0:T(8,128)(2,1)S(1)} copy-done((bf16[3,3,3,128,64]{3,4,2,1,0:T(8,128)(2,1)S(1)}, bf16[3,3,3,128,64]{3,4,2,1,0:T(8,128)(2,1)}, u32[]{:S(2)}) %copy-start.1) | copy-done | bytes 442392
  2.7 0.0 copy-start.2
  2.7 1.0 %copy-done.2 = bf16[3,3,3,64,64]{4,3,2,1,0:T(8,128)(2,1)S(1)} copy-done((bf16[3,3,3,64,64]{4,3,2,1,0:T(8,128)(2,1)S(1)}, bf16[3,3,3,64,64]{4,3,2,1,0:T(8,128)(2,1)}, u32[]{:S(2)}) %copy-start.2) | copy-done | bytes 221208
  3.7 0.0 copy-start.3
  3.7 0.9 %copy-done.3 = bf16[1,1,4,2,64,128]{5,4,3,2,1,0:T(8,128)(2,1)S(1)} copy-done((bf16[1,1,4,2,64,128]{5,4,3,2,1,0:T(8,128)(2,1)S(1)}, bf16[1,1,4,2,64,128]{5,4,3,2,1,0:T(8,128)(2,1)}, u32[]{:S(2)}) %copy-start.3) | copy-done | bytes 131096
  4.6 56.2 %shard_map.75 = (bf16[2048,128]{1,0:T(8,128)(2,1)S(1)}, bf16[512,128]{1,0:T(8,128)(2,1)S(1)}, f32[27,64,64]{2,1,0:T(8,128)S(1)}, f32[1728,128]{1,0:T(8,128)S(1)}) custom-call(bf16[4,2,64,128]{3,2,1,0:T(8,128)(2,1)S(1)} %bitcast.19, bf16[1728,128]{1,0:T(8,128)(2,1)S(1)} %bitcast.17, bf16[1728,64]{1,0:T(8,128)(2,1)S(1)} %bitcast.18, bf16[2048,128]{1,0:T(8,128)(2,1)S(1)} %bitcast.16), custom_call_target="tpu_custom_call" | custom-call | flops 7000000000 | bytes 4000000 | tf_op jit(solution)/shard_map/pallas_call | solution.py:567
  60.8 0.8 %copy.12 = bf16[1,1,64,8,4,128]{5,4,3,2,1,0:T(4,128)(2,1)} copy(bf16[1,1,64,8,4,128]{5,4,3,2,1,0:T(4,128)(2,1)S(1)} %bitcast.14) | data formatting | bytes 1048576
  61.6 0.7 %copy.13 = bf16[1,1,4,2,64,128]{5,4,3,2,1,0:T(8,128)(2,1)} copy(bf16[1,1,4,2,64,128]{5,4,3,2,1,0:T(8,128)(2,1)S(1)} %bitcast.15) | data formatting | bytes 262144
  62.2 0.9 %copy.14 = f32[3,3,3,64,64]{4,3,2,1,0:T(8,128)} copy(f32[3,3,3,64,64]{4,3,2,1,0:T(8,128)S(1)} %bitcast.13) | data formatting | bytes 884736
  63.1 0.9 %copy.15 = f32[3,3,3,128,64]{3,4,2,1,0:T(8,128)} copy(f32[3,3,3,128,64]{3,4,2,1,0:T(8,128)S(1)} %bitcast.12) | data formatting | bytes 1769472
Async XLA Ops:
  0.6 1.0 %copy-start = (bf16[1,1,64,8,4,128]{5,4,3,2,1,0:T(4,128)(2,1)S(1)}, bf16[1,1,64,8,4,128]{5,4,3,2,1,0:T(4,128)(2,1)}, u32[]{:S(2)}) copy-start(bf16[1,1,64,8,4,128]{5,4,3,2,1,0:T(4,128)(2,1)} %param.7) | copy-start | bytes 1572868
  1.7 1.0 %copy-start.1 = (bf16[3,3,3,128,64]{3,4,2,1,0:T(8,128)(2,1)S(1)}, bf16[3,3,3,128,64]{3,4,2,1,0:T(8,128)(2,1)}, u32[]{:S(2)}) copy-start(bf16[3,3,3,128,64]{3,4,2,1,0:T(8,128)(2,1)} %param.5) | copy-start | bytes 1327108
  2.7 1.0 %copy-start.2 = (bf16[3,3,3,64,64]{4,3,2,1,0:T(8,128)(2,1)S(1)}, bf16[3,3,3,64,64]{4,3,2,1,0:T(8,128)(2,1)}, u32[]{:S(2)}) copy-start(bf16[3,3,3,64,64]{4,3,2,1,0:T(8,128)(2,1)} %param.6) | copy-start | bytes 663556
  3.7 0.9 %copy-start.3 = (bf16[1,1,4,2,64,128]{5,4,3,2,1,0:T(8,128)(2,1)S(1)}, bf16[1,1,4,2,64,128]{5,4,3,2,1,0:T(8,128)(2,1)}, u32[]{:S(2)}) copy-start(bf16[1,1,4,2,64,128]{5,4,3,2,1,0:T(8,128)(2,1)} %param.4) | copy-start | bytes 393220

commit v3 on v2

--- a/solution.py
+++ b/solution.py
@@ -17,10 +17,11 @@
 NT = (((1,), (1,)), ((), ()))
 
 DIRS = [(0, 1), (0, -1), (1, 0), (-1, 0), (1, 1), (1, -1), (-1, 1), (-1, -1)]
-COT_Z = {1: (6, 2), 0: (0, 8), -1: (0, 1)}
-COT_Y = {1: (256, 256), 0: (0, 512), -1: (0, 128)}
+COT_Z = {1: (7, 1), 0: (0, 8), -1: (0, 1)}
+COT_Y = {1: (384, 128), 0: (0, 512), -1: (0, 128)}
 COA_Z = {1: (3, 1), 0: (0, 4), -1: (0, 1)}
 COA_Y = {1: (1, 1), 0: (0, 2), -1: (0, 1)}
+BACK = {(0, 1): (4, 64, CIN), (1, 0): (2, 64, CIN), (1, 1): (1, 64, CIN)}
 
 
 def dot(a, b):
@@ -29,10 +30,6 @@
 
 def dot_nt(a, b):
     return lax.dot_general(a, b, NT, preferred_element_type=F32)
-
-
-def mult(n, of):
-    return n
 
 
 def unrolled(start, stop):
@@ -96,7 +93,8 @@
     def __init__(self, at, rows, bufs, sems):
         self.at, self.r = at, rows
         self.v, self.r0, self.s0, self.r1, self.s1, self.r2, self.g = bufs
-        self.pair_sems, self.plane_send, self.plane_recv, self.z_send, self.z_recv, self.back_send, self.back_recv = sems
+        self.pair_sems, self.plane_send, self.plane_recv, self.z_send, self.z_recv, self.back_send, self.back_recv = sems[:7]
+        self.share_send, self.share_recv = sems[7:]
         self.sent = []
 
     def go(self, copy):
@@ -155,15 +153,18 @@
             )
 
     def start_share(self):
-        at = self.at
-        for c in self.c3:
+        at, r = self.at, self.r
+        self.c4 = []
+        for k in range(at.plane):
+            if k:
+                self.c3[k - 1].wait_recv()
+            p = lax.rem(at.p + at.plane - k, at.plane)
+            piece = self.g.at[at.core, pl.ds(pl.multiple_of(p * r, 16), r)]
+            self.c4.append(self.go(remote(piece, piece, self.share_send.at[k], self.share_recv.at[k], at.pair())))
+
+    def finish(self):
+        for c in self.c4:
             c.wait_recv()
-        self.c4 = self.go(
-            remote(self.g.at[at.core], self.g.at[at.core], self.pair_sems.at[2], self.pair_sems.at[3], at.pair())
-        )
-
-    def finish(self):
-        self.c4.wait_recv()
         for c in self.sent:
             c.wait_send()
 
@@ -177,8 +178,8 @@
     cot_hbm,
     field_out,
     gc_out,
-    gcw_out,
-    gtw_out,
+    conv_out,
+    tconv_out,
     coarse,
     tw,
     cw,
@@ -190,10 +191,13 @@
     rest = list(rest)
     cot_halo = {d: rest.pop(0) for d in DIRS}
     coa_halo = {d: rest.pop(0) for d in DIRS}
-    up, w1, w2, w4, w3, act, ds, bb, gh, taps, et, cols, pair_buf = (rest.pop(0) for _ in range(13))
-    bufs = [[rest.pop(0) for _ in range(7)] for _ in range(2)]
-    sems = [[rest.pop(0) for _ in range(7)] for _ in range(2)]
-    load_sem, cot_send, cot_recv, coa_send, coa_recv = rest
+    back_from = {d: rest.pop(0) for d in BACK}
+    back_to = {d: rest.pop(0) for d in BACK}
+    up, w1, w2, w4, w3, act, ds, bb, gh, taps, et, cols, local_gc = (rest.pop(0) for _ in range(13))
+    bufs = [[rest.pop(0) for _ in range(6)] for _ in range(2)]
+    bufs = [b + [out] for b, out in zip(bufs, (conv_out, tconv_out))]
+    sems = [[rest.pop(0) for _ in range(9)] for _ in range(2)]
+    load_sem, cot_send, cot_recv, coa_send, coa_recv, back_send, back_recv = rest
     nz, ny, nx = dims
     at = Place(nz, ny, nx)
 
@@ -216,20 +220,6 @@
     for load in loads:
         load.start()
 
-    loads[0].wait()
-    wide[...] = cot[...].astype(F32)
-    for z in range(8):
-        for y in range(4):
-            rows_cot[z, :, y * 128 : y * 128 + 128] = wide[pl.ds(z * 4 + y, C, stride=32), :].astype(BF16)
-
-    for d in DIRS:
-
-        @pl.when(jnp.logical_not(at.has(-d[0], -d[1])))
-        def _():
-            cot_halo[d][...] = jnp.zeros_like(cot_halo[d])
-            coa_halo[d][...] = jnp.zeros_like(coa_halo[d])
-
-    loads[1].wait()
     count = len(others)
     for d in DIRS:
         count = count + jnp.where(at.has(*d), 1, 0)
@@ -238,7 +228,7 @@
     def coa_copy(i, d):
         (z, dz), (y, dy) = COA_Z[d[0]], COA_Y[d[1]]
         return remote(
-            coarse.at[pl.ds(z, dz), pl.ds(y, dy)], coa_halo[d], coa_send.at[i], coa_recv.at[i], at.halo(*d)
+            coarse_hbm.at[pl.ds(z, dz), pl.ds(y, dy)], coa_halo[d], coa_send.at[i], coa_recv.at[i], at.halo(*d)
         )
 
     def cot_copy(i, d):
@@ -247,19 +237,42 @@
             rows_cot.at[pl.ds(z, dz), :, pl.ds(y, dy)], cot_halo[d], cot_send.at[i], cot_recv.at[i], at.halo(*d)
         )
 
-    for copy_of in (coa_copy, cot_copy):
-        for i, d in enumerate(DIRS):
+    def back_copy(i, d):
+        return remote(back_to[d], back_from[d], back_send.at[i], back_recv.at[i], at.halo(*d))
+
+    def start(copy_of, dirs=DIRS):
+        for i, d in enumerate(dirs):
 
             @pl.when(at.has(*d))
             def _():
                 copy_of(i, d).start()
 
-    def arrived(copy_of):
-        for i, d in enumerate(DIRS):
+    def arrived(copy_of, dirs=DIRS):
+        for i, d in enumerate(dirs):
 
             @pl.when(at.has(-d[0], -d[1]))
             def _():
                 copy_of(i, d).wait_recv()
+
+    start(coa_copy)
+
+    loads[0].wait()
+    wide[...] = cot[...].astype(F32)
+    for z in (0, 7, 1, 2, 3, 4, 5, 6):
+        for y in range(4):
+            rows_cot[z, :, y * 128 : y * 128 + 128] = wide[pl.ds(z * 4 + y, C, stride=32), :].astype(BF16)
+    start(cot_copy)
+
+    for d in DIRS:
+
+        @pl.when(jnp.logical_not(at.has(-d[0], -d[1])))
+        def _():
+            cot_halo[d][...] = jnp.zeros_like(cot_halo[d])
+            coa_halo[d][...] = jnp.zeros_like(coa_halo[d])
+            if d in BACK:
+                back_from[d][...] = jnp.zeros_like(back_from[d])
+
+    loads[1].wait()
 
     loads[2].wait()
     loads[3].wait()
@@ -291,12 +304,12 @@
     def put_cot(ze, ye, row):
         before, row, after = taps_of(row.astype(F32))
         for i, value in enumerate((after, row, before)):
-            bb[pl.ds(mult(ze * 192 + i * C, C), C), ye * 128 : ye * 128 + 128] = value.astype(BF16)
+            bb[pl.ds(ze * 192 + i * C, C), ye * 128 : ye * 128 + 128] = value.astype(BF16)
 
     @unrolled(0, 8)
     def _(z):
         for y in range(4):
-            put_cot(z + 2, y + 2, rows_cot[z, :, y * 128 : y * 128 + 128])
+            put_cot(z + 1, y + 1, rows_cot[z, :, y * 128 : y * 128 + 128])
 
     cell = lax.broadcasted_iota(jnp.int32, (C, 384), 0)
     place = lax.broadcasted_iota(jnp.int32, (C, 384), 1)
@@ -310,7 +323,7 @@
     def put_coarse(ze, ye, block):
         wide_block = dot(block.astype(F32).T.astype(BF16), spread).astype(BF16)
         for k in range(3):
-            up[pl.ds(mult(ze * 384 + k * 128, 128), 128), ye * 128 : ye * 128 + 128] = wide_block[:, k * 128 : k * 128 + 128]
+            up[pl.ds(ze * 384 + k * 128, 128), ye * 128 : ye * 128 + 128] = wide_block[:, k * 128 : k * 128 + 128]
 
     @unrolled(0, 4)
     def _(z):
@@ -335,7 +348,7 @@
     has_yl = jnp.where(at.has_y[-1], 1.0, 0.0).astype(F32)
     has_yh = jnp.where(at.has_y[1], 1.0, 0.0).astype(F32)
 
-    def put_hidden(zf, partial, z_mask, slopes):
+    def put_hidden(zf, partial, z_mask):
         for yf in range(6):
             n = yf // 2
             if yf % 2:
@@ -351,20 +364,19 @@
             if mask is not None:
                 row = row * mask
             for i, value in enumerate(taps_of(row)):
-                act[pl.ds(mult(zf * 192 + i * C, C), C), yf * 128 : yf * 128 + 128] = value.astype(BF16)
-            if yf < 5 and slopes:
-                slope = s * (1.0 + h * (1.0 - s))
-                ds[zf, :, yf * 128 : yf * 128 + 128] = slope if mask is None else slope * mask
+                act[pl.ds(zf * 192 + i * C, C), yf * 128 : yf * 128 + 128] = value.astype(BF16)
+            if 0 < zf < 9 and 0 < yf < 5:
+                ds[zf - 1, :, (yf - 1) * 128 : yf * 128] = s * (1.0 + h * (1.0 - s))
 
     w1_odd = jnp.concatenate([w1[2], w1[0]], axis=1)
 
     @unrolled(0, 5)
     def _(m):
-        start = mult(m * 384, 128)
+        start = m * 384
         odd = dot(w1_odd, up[pl.ds(start, 768), :])
-        put_hidden(2 * m, odd, has_zl if m == 0 else None, True)
-        even = dot(w1[1], up[pl.ds(mult(start + 384, 128), 384), :])
-        put_hidden(2 * m + 1, even, has_zh if m == 4 else None, m < 4)
+        put_hidden(2 * m, odd, has_zl if m == 0 else None)
+        even = dot(w1[1], up[pl.ds(start + 384, 384), :])
+        put_hidden(2 * m + 1, even, has_zh if m == 4 else None)
 
     gc_v, gt_v = bufs[0][0], bufs[1][0]
     conv_sum = Reduction(at, rows_of[0], bufs[0], sems[0])
@@ -374,11 +386,11 @@
     @unrolled(0, 8)
     def _(z):
         blocks = [
-            act[pl.ds(mult((z + dz) * 192 + C, C), C), dy * 128 : dy * 128 + 512]
+            act[pl.ds((z + dz) * 192 + C, C), dy * 128 : dy * 128 + 512]
             for dz in range(3)
             for dy in range(3)
         ]
-        right = bb[pl.ds(mult((z + 2) * 192, C), 192), 256:768]
+        right = bb[pl.ds((z + 1) * 192, 192), 128:640]
         taps[...] += dot_nt(jnp.concatenate(blocks, axis=0), right)
 
     def fill(v, half_rows, parts):
@@ -406,32 +418,30 @@
 
     @unrolled(0, 8)
     def _(z):
-        for y in range(2):
-            put_cot(z + 2, y, cot_halo[(0, 1)][z, :, y * 128 : y * 128 + 128])
-        put_cot(z + 2, 6, cot_halo[(0, -1)][z])
-
-    for dz, planes in ((1, 2), (-1, 1)):
-        for z in range(planes):
-            ze = z if dz > 0 else 10
-            for y in range(2):
-                put_cot(ze, y, cot_halo[(dz, 1)][z, :, y * 128 : y * 128 + 128])
-            for y in range(4):
-                put_cot(ze, y + 2, cot_halo[(dz, 0)][z, :, y * 128 : y * 128 + 128])
-            put_cot(ze, 6, cot_halo[(dz, -1)][z])
+        put_cot(z + 1, 0, cot_halo[(0, 1)][z])
+        put_cot(z + 1, 5, cot_halo[(0, -1)][z])
+
+    for dz, ze in ((1, 0), (-1, 9)):
+        put_cot(ze, 0, cot_halo[(dz, 1)][0])
+        for y in range(4):
+            put_cot(ze, y + 1, cot_halo[(dz, 0)][0, :, y * 128 : y * 128 + 128])
+        put_cot(ze, 5, cot_halo[(dz, -1)][0])
     conv_sum.start_plane()
 
-    @unrolled(0, 9)
-    def _(q):
-        partial = dot(w2[...], bb[pl.ds(mult(q * 192, C), 576), :])
-        for yf in range(5):
-            ga = partial[:C, (yf + 2) * 128 : (yf + 3) * 128]
-            ga = ga + partial[C : 2 * C, (yf + 1) * 128 : (yf + 2) * 128]
-            ga = ga + partial[2 * C :, yf * 128 : yf * 128 + 128]
-            gh[pl.ds(mult(q * C, C), C), yf * 128 : yf * 128 + 128] = (
-                ga * ds[q, :, yf * 128 : yf * 128 + 128]
+    for half in range(2):
+        for q in (0, 9):
+            gh[half, q * C : q * C + C, :] = jnp.zeros((C, 256), BF16)
+
+    @unrolled(0, 8)
+    def _(z):
+        partial = dot(w2[...], bb[pl.ds(z * 192, 576), :])
+        for y in range(4):
+            ga = partial[:C, (y + 2) * 128 : (y + 3) * 128]
+            ga = ga + partial[C : 2 * C, (y + 1) * 128 : (y + 2) * 128]
+            ga = ga + partial[2 * C :, y * 128 : y * 128 + 128]
+            gh[y % 2, (z + 1) * C : (z + 2) * C, y // 2 * 128 : y // 2 * 128 + 128] = (
+                ga * ds[z, :, y * 128 : y * 128 + 128]
             ).astype(BF16)
-
-    conv_sum.start_z()
 
     def picks(shape, f_dim):
         f = lax.broadcasted_iota(jnp.int32, shape, f_dim)
@@ -447,69 +457,140 @@
         return out.astype(BF16)
 
     pick = picks((256, 384), 0)
+    for half in range(2):
+        some = dot(gh[half, C : 9 * C, :], pick).astype(BF16)
+        for z in range(8):
+            for kx in range(3):
+                cols[z % 2, half, kx * C : (kx + 1) * C, z // 2 * 128 : z // 2 * 128 + 128] = some[
+                    z * C : (z + 1) * C, kx * 128 : kx * 128 + 128
+                ]
+
+    def cells(z, y):
+        if z < 4 and y < 2:
+            return coarse[z, y]
+        if z < 4:
+            return coa_halo[(0, -1)][z, 0]
+        return coa_halo[(-1, 0)][0, y] if y < 2 else coa_halo[(-1, -1)][0, 0]
+
+    by_tap = {}
+    for odd_z in range(2):
+        for odd_y in range(2):
+            shifts = [(z, y) for z in range(odd_z + 1) for y in range(odd_y + 1)]
+            right = jnp.concatenate(
+                [
+                    jnp.concatenate([cells(z + sz, y + sy) for z in range(4) for y in range(2)], axis=0)
+                    for sz, sy in shifts
+                ],
+                axis=1,
+            )
+            result = dot(cols[odd_z, odd_y], right)
+            for n, (sz, sy) in enumerate(shifts):
+                kz = 1 if not odd_z else 2 - 2 * sz
+                ky = 1 if not odd_y else 2 - 2 * sy
+                by_tap[kz, ky] = result[:, n * 128 : n * 128 + 128]
+    fill(gt_v, at.plane * rows_of[1], [by_tap[kz, ky] for kz in range(3) for ky in range(3)])
+    tconv_sum.start_pair()
+    conv_sum.start_z()
+
     pick_t = picks((384, 256), 1)
-    for ky in range(3):
-        pair_buf[:, :128] = gh[:, ky * 128 : ky * 128 + 128]
-        pair_buf[:, 128:] = gh[:, (ky + 2) * 128 : (ky + 3) * 128]
-        some = dot(pair_buf[...], pick).astype(BF16)
-        for zc in range(4):
-            for kz in range(3):
-                for kx in range(3):
-                    row = ((kz * 3 + ky) * 3 + kx) * C
-                    q = (2 * zc + kz) * C
-                    cols[row : row + C, zc * 128 : zc * 128 + 128] = some[q : q + C, kx * 128 : kx * 128 + 128]
-        et[ky] = dot_nt(pick_t, pair_buf[...]).astype(BF16)
-
-    fill(gt_v, at.plane * rows_of[1], [dot(cols[...], coarse[...].reshape(512, CIN))])
-    tconv_sum.start_pair()
+    for half in range(2):
+        et[half] = dot_nt(pick_t, gh[half]).astype(BF16)
+
+    def gather(ky, zc):
+        total = None
+        for kx in range(3):
+            rows = slice(kx * 128, kx * 128 + 128)
+            if zc < 4:
+                term = dot(et[int(ky != 1), rows, zc * 128 : zc * 128 + 192], w3[ky * 3 + kx])
+            else:
+                term = dot(et[int(ky != 1), rows, 512:576], w3[ky * 3 + kx, :C, :])
+            total = term if total is None else total + term
+        return total
+
+    for zc in (4, 3, 2, 1, 0):
+        low = gather(1, zc) + gather(2, zc)
+        high = gather(0, zc)
+        rows = (low[:C], low[C:] + high[:C])
+        if zc < 4:
+            for y in range(2):
+                local_gc[zc, y] = rows[y]
+            back_to[(0, 1)][zc] = high[C:].astype(BF16)
+        else:
+            for y in range(2):
+                back_to[(1, 0)][y] = rows[y].astype(BF16)
+            back_to[(1, 1)][0] = high[C:].astype(BF16)
+    tconv_sum.start_plane()
+    start(back_copy, BACK)
     conv_sum.start_back()
 
-    for zc in range(4):
-        total = jnp.zeros((128, CIN), F32)
-        for ky in range(3):
-            for kx in range(3):
-                total = total + dot(et[ky, kx * 128 : kx * 128 + 128, zc * 128 : zc * 128 + 192], w3[ky * 3 + kx])
-        gc_out[zc * 128 : zc * 128 + 128, :] = total.astype(BF16)
-    tconv_sum.start_plane()
-
-    def put_field(z):
-        partial = dot(w4[...], act[pl.ds(mult(z * 192, C), 576), :])
+    @unrolled(0, 8)
+    def _(z):
+        partial = dot(w4[...], act[pl.ds(z * 192, 576), :])
         for y in range(4):
             row = partial[:C, y * 128 : y * 128 + 128]
             row = row + partial[C : 2 * C, (y + 1) * 128 : (y + 2) * 128]
             row = row + partial[2 * C :, (y + 2) * 128 : (y + 3) * 128]
             wide[pl.ds(z * 4 + y, C, stride=32), :] = row
 
-    unrolled(0, 4)(put_field)
+    field_out[...] = wide[...].astype(BF16)
+    tconv_sum.start_z()
     conv_sum.start_share()
-    tconv_sum.start_z()
-    unrolled(4, 8)(put_field)
+
+    arrived(back_copy, BACK)
+    for zc in range(4):
+        for y in range(2):
+            total = local_gc[zc, y]
+            if y == 0:
+                total = total + back_from[(0, 1)][zc].astype(F32)
+            if zc == 0:
+                total = total + back_from[(1, 0)][y].astype(F32)
+            if zc == 0 and y == 0:
+                total = total + back_from[(1, 1)][0].astype(F32)
+            gc_out[zc, y] = total.astype(BF16)
     tconv_sum.start_back()
-    field_out[...] = wide[...].astype(BF16)
-
-    n_dev = nz * ny * nx * 2
     conv_sum.finish()
+    tconv_sum.start_share()
+    tconv_sum.finish()
+
+    def sent(copy_of, dirs=DIRS):
+        for i, d in enumerate(dirs):
+
+            @pl.when(at.has(*d))
+            def _():
+                copy_of(i, d).wait_send()
+
+    sent(coa_copy)
+    sent(cot_copy)
+    sent(back_copy, BACK)
+
+
+def unpack(n_dev, field_in, gc_in, conv_in, tconv_in, field_out, gc_out, gcw_out, gtw_out, conv, tconv, gcw, gtw, sems):
+    copies = [
+        pltpu.make_async_copy(src, dst, sems.at[i])
+        for i, (src, dst) in enumerate(
+            ((conv_in, conv), (tconv_in, tconv), (field_in, field_out), (gc_in, gc_out), (gcw, gcw_out), (gtw, gtw_out))
+        )
+    ]
+    for copy in copies[:4]:
+        copy.start()
+    copies[0].wait()
     conv_scale = 1.0 / math.sqrt(n_dev * 8 * 4 * 128)
-    g = conv_sum.g[...].reshape(-1, 128)
+    g = conv[...].reshape(-1, 128)
     first = g[:576].astype(F32) * conv_scale
     second = g[576:864].astype(F32) * conv_scale
     for zy in range(9):
         for dx in range(2):
-            gcw_out[zy * 3 + dx] = first[zy * C : (zy + 1) * C, dx * C : (dx + 1) * C]
+            gcw[zy * 3 + dx] = first[zy * C : (zy + 1) * C, dx * C : (dx + 1) * C]
     for half in range(18):
         src = second[(half % 9) * 32 : (half % 9) * 32 + 32, (half // 9) * C : (half // 9 + 1) * C]
-        gcw_out[(half // 2) * 3 + 2, (half % 2) * 32 : (half % 2) * 32 + 32, :] = src
-    tconv_sum.start_share()
-    tconv_sum.finish()
+        gcw[(half // 2) * 3 + 2, (half % 2) * 32 : (half % 2) * 32 + 32, :] = src
+    copies[4].start()
+    copies[1].wait()
     tconv_scale = 1.0 / math.sqrt(n_dev * 4 * 2 * 64)
-    gtw_out[...] = tconv_sum.g[...].reshape(-1, 128)[:1728].astype(F32) * tconv_scale
-
-    for copy_of in (coa_copy, cot_copy):
-        for i, d in enumerate(DIRS):
-
-            @pl.when(at.has(*d))
-            def _():
-                copy_of(i, d).wait_send()
+    gtw[...] = tconv[...].reshape(-1, 128)[:1728].astype(F32) * tconv_scale
+    copies[5].start()
+    for copy in copies[2:]:
+        copy.wait()
 
 
 def solution(mesh):
@@ -533,6 +614,7 @@
         ]
         scratch += [vmem((COT_Z[dz][1], C, COT_Y[dy][1]), BF16) for dz, dy in DIRS]
         scratch += [vmem((COA_Z[dz][1], COA_Y[dy][1], 64, CIN), BF16) for dz, dy in DIRS]
+        scratch += [vmem(shape, BF16) for shape in BACK.values()] * 2
         scratch += [
             vmem((6 * 384, 512), BF16),
             vmem((3, 192, 384), BF16),
@@ -540,13 +622,13 @@
             vmem((192, 576), BF16),
             vmem((9, 192, CIN), BF16),
             vmem((10 * 192, 768), BF16),
-            vmem((9, C, 640), F32),
-            vmem((11 * 192, 896), BF16),
-            vmem((9 * C, 640), BF16),
+            vmem((8, C, 512), F32),
+            vmem((10 * 192, 768), BF16),
+            vmem((2, 10 * C, 256), BF16),
             vmem((576, 192), F32),
-            vmem((3, 384, 576), BF16),
-            vmem((1728, 512), BF16),
-            vmem((576, 256), BF16),
+            vmem((2, 384, 640), BF16),
+            vmem((2, 2, 192, 512), BF16),
+            vmem((4, 2, 64, CIN), F32),
         ]
         for r in rows_of:
             scratch += [
@@ -556,27 +638,26 @@
                 vmem((plane - 1, r, 128), BF16),
                 vmem((r, 128), BF16),
                 vmem((nz, r, 128), BF16),
-                vmem((2, plane * r, 128), BF16),
             ]
         for r in rows_of:
-            scratch += [dma((4,)), dma((plane - 1,)), dma((plane - 1,)), dma((nz - 1,)), dma((nz - 1,))]
-            scratch += [dma((plane - 1,)), dma((plane - 1,))]
-        scratch += [dma((4,)), dma((8,)), dma((8,)), dma((8,)), dma((8,))]
-        any_space = pl.BlockSpec(memory_space=pl.ANY)
+            scratch += [dma((2,)), dma((plane - 1,)), dma((plane - 1,)), dma((nz - 1,)), dma((nz - 1,))]
+            scratch += [dma((plane - 1,)), dma((plane - 1,)), dma((plane,)), dma((plane,))]
+        scratch += [dma((4,)), dma((8,)), dma((8,)), dma((8,)), dma((8,)), dma((3,)), dma((3,))]
+        in_hbm = pl.BlockSpec(memory_space=pltpu.HBM)
         in_vmem = pl.BlockSpec(memory_space=pltpu.VMEM)
-        field, gc, gcw, gtw = pl.pallas_call(
+        parts = pl.pallas_call(
             functools.partial(kernel, (nz, ny, nx), rows_of),
             out_shape=(
                 jax.ShapeDtypeStruct((2048, 128), BF16),
-                jax.ShapeDtypeStruct((512, CIN), BF16),
-                jax.ShapeDtypeStruct((27, C, C), F32),
-                jax.ShapeDtypeStruct((27 * C, CIN), F32),
+                jax.ShapeDtypeStruct((4, 2, 64, CIN), BF16),
+                jax.ShapeDtypeStruct((2, plane * rows_of[0], 128), BF16),
+                jax.ShapeDtypeStruct((2, plane * rows_of[1], 128), BF16),
             ),
-            in_specs=[any_space] * 4,
+            in_specs=[in_hbm] * 4,
             out_specs=(in_vmem,) * 4,
             scratch_shapes=scratch,
             compiler_params=pltpu.CompilerParams(
-                collective_id=0, has_side_effects=True, vmem_limit_bytes=50 * 2**20
+                collective_id=0, has_side_effects=True, vmem_limit_bytes=61 * 2**20
             ),
             cost_estimate=pl.CostEstimate(flops=7 * 10**9, bytes_accessed=4 * 10**6, transcendentals=500000),
         )(
@@ -585,6 +666,26 @@
             cw.reshape(27 * C, C),
             cot.reshape(2048, 128),
         )
+        any_space = pl.BlockSpec(memory_space=pl.ANY)
+        field, gc, gcw, gtw = pl.pallas_call(
+            functools.partial(unpack, n_slab * nx),
+            out_shape=(
+                jax.ShapeDtypeStruct((2048, 128), BF16),
+                jax.ShapeDtypeStruct((4, 2, 64, CIN), BF16),
+                jax.ShapeDtypeStruct((27, C, C), F32),
+                jax.ShapeDtypeStruct((27 * C, CIN), F32),
+            ),
+            in_specs=[any_space] * 4,
+            out_specs=(any_space,) * 4,
+            scratch_shapes=[
+                vmem(parts[2].shape, BF16),
+                vmem(parts[3].shape, BF16),
+                vmem((27, C, C), F32),
+                vmem((27 * C, CIN), F32),
+                dma((6,)),
+            ],
+            compiler_params=pltpu.CompilerParams(vmem_limit_bytes=61 * 2**20),
+        )(*parts)
         return (
             field.reshape(1, 1, C, 8, 4, 128),
             gc.reshape(1, 1, 4, 2, 64, CIN),

time: 64.3 us -> 74.2 us (1.15)
  Pallas kernels: 56.2 us -> 73.4 us
  local copies, waits for them, and re-layouts: 7.24 us -> 0 us
    pallas_call x0 -> x1, Pallas kernels: none -> 21 us  [step(): pl.pallas_call(functools.partial(unpack, n_slab * nx), out_shape=(jax.Sha...]
    unnamed x12 -> x0, local copies, waits for them, and re-layouts: 7.24 us -> none
    pallas_call x1, Pallas kernels: 56.2 us -> 52.4 us  [step(): pl.pallas_call(functools.partial(kernel, (nz, ny, nx), rows_of), out_shap...]
where the time goes in v3:
time: 74.2 us; the launch traced here: 74.1 us
  Pallas kernels  73.4 us (99%)
    pallas_call x1, Pallas kernels, step(): pl.pallas_call(functools.partial(kernel, (nz, ny, nx), rows_of), out_shap...  52.4 us
    pallas_call x1, Pallas kernels, step(): pl.pallas_call(functools.partial(unpack, n_slab * nx), out_shape=(jax.Sha...  21 us

profile of v3, /device:TPU:1, one launch (start us, length us, event | category | flops | bytes accessed | tf_op | source)
XLA Modules:
  0.0 74.1 jit_solution(9185984595393308893)
XLA Ops:
  0.6 52.4 %shard_map.75 = (bf16[2048,128]{1,0:T(8,128)(2,1)}, bf16[4,2,64,128]{3,2,1,0:T(8,128)(2,1)}, bf16[2,512,128]{2,1,0:T(8,128)(2,1)}, bf16[2,1024,128]{2,1,0:T(8,128)(2,1)}) custom-call(bf16[4,2,64,128]{3,2,1,0:T(8,128)(2,1)} %bitcast.18, bf16[1728,128]{1,0:T(8,128)(2,1)} %bitcast.16, bf16[1728,64]{1,0:T(8,128)(2,1)} %bitcast.17, bf16[2048,128]{1,0:T(8,128)(2,1)} %bitcast.14), custom_call_target="tpu_custom_call" | custom-call | flops 7000000000 | bytes 4000000 | tf_op jit(solution)/shard_map/pallas_call | solution.py:648
  53.1 21.0 %shard_map.76 = (bf16[2048,128]{1,0:T(8,128)(2,1)}, bf16[4,2,64,128]{3,2,1,0:T(8,128)(2,1)}, f32[27,64,64]{2,1,0:T(8,128)}, f32[1728,128]{1,0:T(8,128)}) custom-call(bf16[2048,128]{1,0:T(8,128)(2,1)} %get-tuple-element.12.field_in, bf16[4,2,64,128]{3,2,1,0:T(8,128)(2,1)} %get-tuple-element.13.gc_in, bf16[2,512,128]{2,1,0:T(8,128)(2,1)} %get-tuple-element.14.conv_in, ...), custom_call_target="tpu_custom_call" | custom-call | tf_op jit(solution)/shard_map/pallas_call | solution.py:670

commit v4 on v3

--- a/solution.py
+++ b/solution.py
@@ -564,16 +564,17 @@
     sent(back_copy, BACK)
 
 
-def unpack(n_dev, field_in, gc_in, conv_in, tconv_in, field_out, gc_out, gcw_out, gtw_out, conv, tconv, gcw, gtw, sems):
-    copies = [
-        pltpu.make_async_copy(src, dst, sems.at[i])
-        for i, (src, dst) in enumerate(
-            ((conv_in, conv), (tconv_in, tconv), (field_in, field_out), (gc_in, gc_out), (gcw, gcw_out), (gtw, gtw_out))
-        )
+def unpack(n_dev, *refs):
+    ins, outs, held, (gcw, gtw), (sems,) = refs[:4], refs[4:8], refs[8:12], refs[12:14], refs[14:]
+    loads = [pltpu.make_async_copy(src, dst, sems.at[i]) for i, (src, dst) in enumerate(zip(ins, held))]
+    stores = [
+        pltpu.make_async_copy(src, dst, sems.at[4 + i])
+        for i, (src, dst) in enumerate(zip((held[0], held[1], gcw, gtw), outs))
     ]
-    for copy in copies[:4]:
-        copy.start()
-    copies[0].wait()
+    for i in (2, 3, 0, 1):
+        loads[i].start()
+    conv, tconv = held[2:]
+    loads[2].wait()
     conv_scale = 1.0 / math.sqrt(n_dev * 8 * 4 * 128)
     g = conv[...].reshape(-1, 128)
     first = g[:576].astype(F32) * conv_scale
@@ -584,13 +585,16 @@
     for half in range(18):
         src = second[(half % 9) * 32 : (half % 9) * 32 + 32, (half // 9) * C : (half // 9 + 1) * C]
         gcw[(half // 2) * 3 + 2, (half % 2) * 32 : (half % 2) * 32 + 32, :] = src
-    copies[4].start()
-    copies[1].wait()
+    stores[2].start()
+    loads[3].wait()
     tconv_scale = 1.0 / math.sqrt(n_dev * 4 * 2 * 64)
     gtw[...] = tconv[...].reshape(-1, 128)[:1728].astype(F32) * tconv_scale
-    copies[5].start()
-    for copy in copies[2:]:
-        copy.wait()
+    stores[3].start()
+    for i in range(2):
+        loads[i].wait()
+        stores[i].start()
+    for store in stores:
+        store.wait()
 
 
 def solution(mesh):
@@ -678,11 +682,10 @@
             in_specs=[any_space] * 4,
             out_specs=(any_space,) * 4,
             scratch_shapes=[
-                vmem(parts[2].shape, BF16),
-                vmem(parts[3].shape, BF16),
+                *(vmem(part.shape, BF16) for part in parts),
                 vmem((27, C, C), F32),
                 vmem((27 * C, CIN), F32),
-                dma((6,)),
+                dma((8,)),
             ],
             compiler_params=pltpu.CompilerParams(vmem_limit_bytes=61 * 2**20),
         )(*parts)

time: 74.2 us -> 55.8 us (0.75)
  Pallas kernels: 73.4 us -> 55 us
    pallas_call x1, Pallas kernels: 21 us -> 2.62 us  [step(): pl.pallas_call(functools.partial(unpack, n_slab * nx), out_shape=(jax.Sha...]
where the time goes in v4:
time: 55.8 us; the launch traced here: 55.7 us
  Pallas kernels  55 us (99%)
  between operations  0.64 us (1%)
    pallas_call x1, Pallas kernels, step(): pl.pallas_call(functools.partial(kernel, (nz, ny, nx), rows_of), out_shap...  52.4 us
    pallas_call x1, Pallas kernels, step(): pl.pallas_call(functools.partial(unpack, n_slab * nx), out_shape=(jax.Sha...  2.62 us

profile of v4, /device:TPU:1, one launch (start us, length us, event | category | flops | bytes accessed | tf_op | source)
XLA Modules:
  0.0 55.7 jit_solution(14309925859971730208)
XLA Ops:
  0.6 52.4 %shard_map.75 = (bf16[2048,128]{1,0:T(8,128)(2,1)}, bf16[4,2,64,128]{3,2,1,0:T(8,128)(2,1)}, bf16[2,512,128]{2,1,0:T(8,128)(2,1)}, bf16[2,1024,128]{2,1,0:T(8,128)(2,1)}) custom-call(bf16[4,2,64,128]{3,2,1,0:T(8,128)(2,1)} %bitcast.18, bf16[1728,128]{1,0:T(8,128)(2,1)} %bitcast.16, bf16[1728,64]{1,0:T(8,128)(2,1)} %bitcast.17, bf16[2048,128]{1,0:T(8,128)(2,1)} %bitcast.14), custom_call_target="tpu_custom_call" | custom-call | flops 7000000000 | bytes 4000000 | tf_op jit(solution)/shard_map/pallas_call | solution.py:652
  53.1 2.6 %shard_map.76 = (bf16[2048,128]{1,0:T(8,128)(2,1)}, bf16[4,2,64,128]{3,2,1,0:T(8,128)(2,1)}, f32[27,64,64]{2,1,0:T(8,128)}, f32[1728,128]{1,0:T(8,128)}) custom-call(bf16[2048,128]{1,0:T(8,128)(2,1)} %get-tuple-element.12.refs_0_, bf16[4,2,64,128]{3,2,1,0:T(8,128)(2,1)} %get-tuple-element.13.refs_1_, bf16[2,512,128]{2,1,0:T(8,128)(2,1)} %get-tuple-element.14.refs_2_, ...), custom_call_target="tpu_custom_call" | custom-call | tf_op jit(solution)/shard_map/pallas_call | solution.py:674

commit v5 on v4

--- a/solution.py
+++ b/solution.py
@@ -220,6 +220,11 @@
     for load in loads:
         load.start()
 
+    loads[0].wait()
+    wide[...] = cot[...].astype(F32)
+    for z in (0, 7, 1, 2, 3, 4, 5, 6):
+        for y in range(4):
+            rows_cot[z, :, y * 128 : y * 128 + 128] = wide[pl.ds(z * 4 + y, C, stride=32), :].astype(BF16)
     count = len(others)
     for d in DIRS:
         count = count + jnp.where(at.has(*d), 1, 0)
@@ -256,11 +261,6 @@
 
     start(coa_copy)
 
-    loads[0].wait()
-    wide[...] = cot[...].astype(F32)
-    for z in (0, 7, 1, 2, 3, 4, 5, 6):
-        for y in range(4):
-            rows_cot[z, :, y * 128 : y * 128 + 128] = wide[pl.ds(z * 4 + y, C, stride=32), :].astype(BF16)
     start(cot_copy)
 
     for d in DIRS:
@@ -282,18 +282,6 @@
                 block = tw[((kz * 3 + ky) * 3 + kx) * C : ((kz * 3 + ky) * 3 + kx + 1) * C, :]
                 w1[kz, ky * C : (ky + 1) * C, kx * 128 : kx * 128 + 128] = block
                 w3[ky * 3 + kx, kz * C : (kz + 1) * C, :] = block
-    for a in range(3):
-        tall = jnp.concatenate([cw[(b * 3 + a) * 192 : (b * 3 + a + 1) * 192, :].astype(F32) for b in range(3)], axis=0)
-        w4[a * C : (a + 1) * C, :] = tall.T.astype(BF16)
-        w2[a * C : (a + 1) * C, :] = jnp.concatenate(
-            [
-                cw[((b * 3 + a) * 3 + x) * C : ((b * 3 + a) * 3 + x + 1) * C, :].astype(F32)
-                for b in (2, 1, 0)
-                for x in range(3)
-            ],
-            axis=1,
-        ).astype(BF16)
-
     lane_at = lax.broadcasted_iota(jnp.int32, (C, 128), 1)
     not_first = jnp.where(lane_at == 0, 0.0, 1.0).astype(F32)
     not_last = jnp.where(lane_at == 127, 0.0, 1.0).astype(F32)
@@ -414,6 +402,19 @@
     )
     conv_sum.start_pair()
 
+    for a in range(3):
+        tall = jnp.concatenate([cw[(b * 3 + a) * 192 : (b * 3 + a + 1) * 192, :].astype(F32) for b in range(3)], axis=0)
+        w4[a * C : (a + 1) * C, :] = tall.T.astype(BF16)
+        w2[a * C : (a + 1) * C, :] = jnp.concatenate(
+            [
+                cw[((b * 3 + a) * 3 + x) * C : ((b * 3 + a) * 3 + x + 1) * C, :].astype(F32)
+                for b in (2, 1, 0)
+                for x in range(3)
+            ],
+            axis=1,
+        ).astype(BF16)
+    conv_sum.start_plane()
+
     arrived(cot_copy)
 
     @unrolled(0, 8)
@@ -426,7 +427,6 @@
         for y in range(4):
             put_cot(ze, y + 1, cot_halo[(dz, 0)][0, :, y * 128 : y * 128 + 128])
         put_cot(ze, 5, cot_halo[(dz, -1)][0])
-    conv_sum.start_plane()
 
     for half in range(2):
         for q in (0, 9):
@@ -490,7 +490,6 @@
                 by_tap[kz, ky] = result[:, n * 128 : n * 128 + 128]
     fill(gt_v, at.plane * rows_of[1], [by_tap[kz, ky] for kz in range(3) for ky in range(3)])
     tconv_sum.start_pair()
-    conv_sum.start_z()
 
     pick_t = picks((384, 256), 1)
     for half in range(2):
@@ -520,8 +519,8 @@
                 back_to[(1, 0)][y] = rows[y].astype(BF16)
             back_to[(1, 1)][0] = high[C:].astype(BF16)
     tconv_sum.start_plane()
+    conv_sum.start_z()
     start(back_copy, BACK)
-    conv_sum.start_back()
 
     @unrolled(0, 8)
     def _(z):
@@ -534,7 +533,7 @@
 
     field_out[...] = wide[...].astype(BF16)
     tconv_sum.start_z()
-    conv_sum.start_share()
+    conv_sum.start_back()
 
     arrived(back_copy, BACK)
     for zc in range(4):
@@ -548,20 +547,21 @@
                 total = total + back_from[(1, 1)][0].astype(F32)
             gc_out[zc, y] = total.astype(BF16)
     tconv_sum.start_back()
+    conv_sum.start_share()
+
+    def sent(copy_of, dirs=DIRS):
+        for i, d in enumerate(dirs):
+
+            @pl.when(at.has(*d))
+            def _():
+                copy_of(i, d).wait_send()
+
+    sent(coa_copy)
+    sent(cot_copy)
+    sent(back_copy, BACK)
     conv_sum.finish()
     tconv_sum.start_share()
     tconv_sum.finish()
-
-    def sent(copy_of, dirs=DIRS):
-        for i, d in enumerate(dirs):
-
-            @pl.when(at.has(*d))
-            def _():
-                copy_of(i, d).wait_send()
-
-    sent(coa_copy)
-    sent(cot_copy)
-    sent(back_copy, BACK)
 
 
 def unpack(n_dev, *refs):

time: 55.8 us -> 53.6 us (0.961)
  Pallas kernels: 55 us -> 52.8 us
    pallas_call x1, Pallas kernels: 52.4 us -> 50.2 us  [step(): pl.pallas_call(functools.partial(kernel, (nz, ny, nx), rows_of), out_shap...]
where the time goes in v5:
time: 53.6 us; the launch traced here: 53.5 us
  Pallas kernels  52.8 us (99%)
  between operations  0.64 us (1%)
    pallas_call x1, Pallas kernels, step(): pl.pallas_call(functools.partial(kernel, (nz, ny, nx), rows_of), out_shap...  50.2 us
    pallas_call x1, Pallas kernels, step(): pl.pallas_call(functools.partial(unpack, n_slab * nx), out_shape=(jax.Sha...  2.62 us

profile of v5, /device:TPU:1, one launch (start us, length us, event | category | flops | bytes accessed | tf_op | source)
XLA Modules:
  0.0 53.5 jit_solution(1640014902320976560)
XLA Ops:
  0.6 50.2 %shard_map.75 = (bf16[2048,128]{1,0:T(8,128)(2,1)}, bf16[4,2,64,128]{3,2,1,0:T(8,128)(2,1)}, bf16[2,512,128]{2,1,0:T(8,128)(2,1)}, bf16[2,1024,128]{2,1,0:T(8,128)(2,1)}) custom-call(bf16[4,2,64,128]{3,2,1,0:T(8,128)(2,1)} %bitcast.18, bf16[1728,128]{1,0:T(8,128)(2,1)} %bitcast.16, bf16[1728,64]{1,0:T(8,128)(2,1)} %bitcast.17, bf16[2048,128]{1,0:T(8,128)(2,1)} %bitcast.14), custom_call_target="tpu_custom_call" | custom-call | flops 7000000000 | bytes 4000000 | tf_op jit(solution)/shard_map/pallas_call | solution.py:652
  50.8 2.6 %shard_map.76 = (bf16[2048,128]{1,0:T(8,128)(2,1)}, bf16[4,2,64,128]{3,2,1,0:T(8,128)(2,1)}, f32[27,64,64]{2,1,0:T(8,128)}, f32[1728,128]{1,0:T(8,128)}) custom-call(bf16[2048,128]{1,0:T(8,128)(2,1)} %get-tuple-element.12.refs_0_, bf16[4,2,64,128]{3,2,1,0:T(8,128)(2,1)} %get-tuple-element.13.refs_1_, bf16[2,512,128]{2,1,0:T(8,128)(2,1)} %get-tuple-element.14.refs_2_, ...), custom_call_target="tpu_custom_call" | custom-call | tf_op jit(solution)/shard_map/pallas_call | solution.py:674

commit v6 on v5

--- a/solution.py
+++ b/solution.py
@@ -17,6 +17,7 @@
 NT = (((1,), (1,)), ((), ()))
 
 DIRS = [(0, 1), (0, -1), (1, 0), (-1, 0), (1, 1), (1, -1), (-1, 1), (-1, -1)]
+NEAR, FAR = DIRS[:2], DIRS[2:]
 COT_Z = {1: (7, 1), 0: (0, 8), -1: (0, 1)}
 COT_Y = {1: (384, 128), 0: (0, 512), -1: (0, 128)}
 COA_Z = {1: (3, 1), 0: (0, 4), -1: (0, 1)}
@@ -162,9 +163,11 @@
             piece = self.g.at[at.core, pl.ds(pl.multiple_of(p * r, 16), r)]
             self.c4.append(self.go(remote(piece, piece, self.share_send.at[k], self.share_recv.at[k], at.pair())))
 
-    def finish(self):
+    def arrive(self):
         for c in self.c4:
             c.wait_recv()
+
+    def finish(self):
         for c in self.sent:
             c.wait_send()
 
@@ -194,10 +197,10 @@
     back_from = {d: rest.pop(0) for d in BACK}
     back_to = {d: rest.pop(0) for d in BACK}
     up, w1, w2, w4, w3, act, ds, bb, gh, taps, et, cols, local_gc = (rest.pop(0) for _ in range(13))
-    bufs = [[rest.pop(0) for _ in range(6)] for _ in range(2)]
-    bufs = [b + [out] for b, out in zip(bufs, (conv_out, tconv_out))]
+    bufs = [[rest.pop(0) for _ in range(7)] for _ in range(2)]
+    field, gc = rest.pop(0), rest.pop(0)
     sems = [[rest.pop(0) for _ in range(9)] for _ in range(2)]
-    load_sem, cot_send, cot_recv, coa_send, coa_recv, back_send, back_recv = rest
+    load_sem, cot_send, cot_recv, coa_send, coa_recv, back_send, back_recv, out_sem = rest
     nz, ny, nx = dims
     at = Place(nz, ny, nx)
 
@@ -257,7 +260,7 @@
 
             @pl.when(at.has(-d[0], -d[1]))
             def _():
-                copy_of(i, d).wait_recv()
+                copy_of(i + (2 if dirs is FAR else 0), d).wait_recv()
 
     start(coa_copy)
 
@@ -318,18 +321,12 @@
         for y in range(2):
             put_coarse(z + 1, y + 1, coarse[z, y])
 
-    arrived(coa_copy)
+    arrived(coa_copy, NEAR)
 
     @unrolled(0, 4)
     def _(z):
         put_coarse(z + 1, 0, coa_halo[(0, 1)][z, 0])
         put_coarse(z + 1, 3, coa_halo[(0, -1)][z, 0])
-
-    for dz, ze in ((1, 0), (-1, 5)):
-        put_coarse(ze, 0, coa_halo[(dz, 1)][0, 0])
-        for y in range(2):
-            put_coarse(ze, y + 1, coa_halo[(dz, 0)][0, y])
-        put_coarse(ze, 3, coa_halo[(dz, -1)][0, 0])
 
     has_zl = jnp.where(at.has_z[-1], 1.0, 0.0).astype(F32)
     has_zh = jnp.where(at.has_z[1], 1.0, 0.0).astype(F32)
@@ -358,13 +355,27 @@
 
     w1_odd = jnp.concatenate([w1[2], w1[0]], axis=1)
 
-    @unrolled(0, 5)
-    def _(m):
-        start = m * 384
-        odd = dot(w1_odd, up[pl.ds(start, 768), :])
-        put_hidden(2 * m, odd, has_zl if m == 0 else None)
-        even = dot(w1[1], up[pl.ds(start + 384, 384), :])
-        put_hidden(2 * m + 1, even, has_zh if m == 4 else None)
+    def odd_plane(m, z_mask=None):
+        put_hidden(2 * m, dot(w1_odd, up[m * 384 : m * 384 + 768, :]), z_mask)
+
+    def even_plane(m, z_mask=None):
+        put_hidden(2 * m + 1, dot(w1[1], up[(m + 1) * 384 : (m + 2) * 384, :]), z_mask)
+
+    for m in range(4):
+        if m:
+            odd_plane(m)
+        even_plane(m)
+
+    arrived(coa_copy, FAR)
+    for dz, ze in ((1, 0), (-1, 5)):
+        put_coarse(ze, 0, coa_halo[(dz, 1)][0, 0])
+        for y in range(2):
+            put_coarse(ze, y + 1, coa_halo[(dz, 0)][0, y])
+        put_coarse(ze, 3, coa_halo[(dz, -1)][0, 0])
+
+    odd_plane(0, has_zl)
+    odd_plane(4)
+    even_plane(4, has_zh)
 
     gc_v, gt_v = bufs[0][0], bufs[1][0]
     conv_sum = Reduction(at, rows_of[0], bufs[0], sems[0])
@@ -415,25 +426,18 @@
         ).astype(BF16)
     conv_sum.start_plane()
 
-    arrived(cot_copy)
+    arrived(cot_copy, NEAR)
 
     @unrolled(0, 8)
     def _(z):
         put_cot(z + 1, 0, cot_halo[(0, 1)][z])
         put_cot(z + 1, 5, cot_halo[(0, -1)][z])
 
-    for dz, ze in ((1, 0), (-1, 9)):
-        put_cot(ze, 0, cot_halo[(dz, 1)][0])
-        for y in range(4):
-            put_cot(ze, y + 1, cot_halo[(dz, 0)][0, :, y * 128 : y * 128 + 128])
-        put_cot(ze, 5, cot_halo[(dz, -1)][0])
-
     for half in range(2):
         for q in (0, 9):
             gh[half, q * C : q * C + C, :] = jnp.zeros((C, 256), BF16)
 
-    @unrolled(0, 8)
-    def _(z):
+    def grad_plane(z):
         partial = dot(w2[...], bb[pl.ds(z * 192, 576), :])
         for y in range(4):
             ga = partial[:C, (y + 2) * 128 : (y + 3) * 128]
@@ -442,6 +446,16 @@
             gh[y % 2, (z + 1) * C : (z + 2) * C, y // 2 * 128 : y // 2 * 128 + 128] = (
                 ga * ds[z, :, y * 128 : y * 128 + 128]
             ).astype(BF16)
+
+    unrolled(1, 7)(grad_plane)
+    arrived(cot_copy, FAR)
+    for dz, ze in ((1, 0), (-1, 9)):
+        put_cot(ze, 0, cot_halo[(dz, 1)][0])
+        for y in range(4):
+            put_cot(ze, y + 1, cot_halo[(dz, 0)][0, :, y * 128 : y * 128 + 128])
+        put_cot(ze, 5, cot_halo[(dz, -1)][0])
+    grad_plane(0)
+    grad_plane(7)
 
     def picks(shape, f_dim):
         f = lax.broadcasted_iota(jnp.int32, shape, f_dim)
@@ -531,7 +545,9 @@
             row = row + partial[2 * C :, (y + 2) * 128 : (y + 3) * 128]
             wide[pl.ds(z * 4 + y, C, stride=32), :] = row
 
-    field_out[...] = wide[...].astype(BF16)
+    field[...] = wide[...].astype(BF16)
+    outs = [pltpu.make_async_copy(field, field_out, out_sem.at[0]), pltpu.make_async_copy(gc, gc_out, out_sem.at[1])]
+    outs[0].start()
     tconv_sum.start_z()
     conv_sum.start_back()
 
@@ -545,7 +561,8 @@
                 total = total + back_from[(1, 0)][y].astype(F32)
             if zc == 0 and y == 0:
                 total = total + back_from[(1, 1)][0].astype(F32)
-            gc_out[zc, y] = total.astype(BF16)
+            gc[zc, y] = total.astype(BF16)
+    outs[1].start()
     tconv_sum.start_back()
     conv_sum.start_share()
 
@@ -559,9 +576,21 @@
     sent(coa_copy)
     sent(cot_copy)
     sent(back_copy, BACK)
+    for i, (total, out) in enumerate(((conv_sum, conv_out), (tconv_sum, tconv_out))):
+        if total is tconv_sum:
+            total.start_share()
+        halves = [
+            pltpu.make_async_copy(total.g.at[h], out.at[h], out_sem.at[2 * i + 2 + n])
+            for n, h in enumerate((at.core, 1 - at.core))
+        ]
+        halves[0].start()
+        total.arrive()
+        halves[1].start()
+        outs += halves
     conv_sum.finish()
-    tconv_sum.start_share()
     tconv_sum.finish()
+    for copy in outs:
+        copy.wait()
 
 
 def unpack(n_dev, *refs):
@@ -642,13 +671,14 @@
                 vmem((plane - 1, r, 128), BF16),
                 vmem((r, 128), BF16),
                 vmem((nz, r, 128), BF16),
+                vmem((2, plane * r, 128), BF16),
             ]
+        scratch += [vmem((2048, 128), BF16), vmem((4, 2, 64, CIN), BF16)]
         for r in rows_of:
             scratch += [dma((2,)), dma((plane - 1,)), dma((plane - 1,)), dma((nz - 1,)), dma((nz - 1,))]
             scratch += [dma((plane - 1,)), dma((plane - 1,)), dma((plane,)), dma((plane,))]
-        scratch += [dma((4,)), dma((8,)), dma((8,)), dma((8,)), dma((8,)), dma((3,)), dma((3,))]
+        scratch += [dma((4,)), dma((8,)), dma((8,)), dma((8,)), dma((8,)), dma((3,)), dma((3,)), dma((6,))]
         in_hbm = pl.BlockSpec(memory_space=pltpu.HBM)
-        in_vmem = pl.BlockSpec(memory_space=pltpu.VMEM)
         parts = pl.pallas_call(
             functools.partial(kernel, (nz, ny, nx), rows_of),
             out_shape=(
@@ -658,7 +688,7 @@
                 jax.ShapeDtypeStruct((2, plane * rows_of[1], 128), BF16),
             ),
             in_specs=[in_hbm] * 4,
-            out_specs=(in_vmem,) * 4,
+            out_specs=(in_hbm,) * 4,
             scratch_shapes=scratch,
             compiler_params=pltpu.CompilerParams(
                 collective_id=0, has_side_effects=True, vmem_limit_bytes=61 * 2**20

time: 53.6 us -> 52.4 us (0.978)
  Pallas kernels: 52.8 us -> 51.6 us
    pallas_call x1, Pallas kernels: 50.2 us -> 49 us  [step(): pl.pallas_call(functools.partial(kernel, (nz, ny, nx), rows_of), out_shap...]
where the time goes in v6:
time: 52.4 us; the launch traced here: 52.2 us
  Pallas kernels  51.6 us (98%)
  between operations  0.64 us (1%)
    pallas_call x1, Pallas kernels, step(): pl.pallas_call(functools.partial(kernel, (nz, ny, nx), rows_of), out_shap...  49 us
    pallas_call x1, Pallas kernels, step(): pl.pallas_call(functools.partial(unpack, n_slab * nx), out_shape=(jax.Sha...  2.62 us

profile of v6, /device:TPU:1, one launch (start us, length us, event | category | flops | bytes accessed | tf_op | source)
XLA Modules:
  0.0 52.2 jit_solution(319502812451746841)
XLA Ops:
  0.6 49.0 %shard_map.75 = (bf16[2048,128]{1,0:T(8,128)(2,1)}, bf16[4,2,64,128]{3,2,1,0:T(8,128)(2,1)}, bf16[2,512,128]{2,1,0:T(8,128)(2,1)}, bf16[2,1024,128]{2,1,0:T(8,128)(2,1)}) custom-call(bf16[4,2,64,128]{3,2,1,0:T(8,128)(2,1)} %bitcast.18, bf16[1728,128]{1,0:T(8,128)(2,1)} %bitcast.16, bf16[1728,64]{1,0:T(8,128)(2,1)} %bitcast.17, bf16[2048,128]{1,0:T(8,128)(2,1)} %bitcast.14), custom_call_target="tpu_custom_call" | custom-call | flops 7000000000 | bytes 4000000 | tf_op jit(solution)/shard_map/pallas_call | solution.py:682
  49.6 2.6 %shard_map.76 = (bf16[2048,128]{1,0:T(8,128)(2,1)}, bf16[4,2,64,128]{3,2,1,0:T(8,128)(2,1)}, f32[27,64,64]{2,1,0:T(8,128)}, f32[1728,128]{1,0:T(8,128)}) custom-call(bf16[2048,128]{1,0:T(8,128)(2,1)} %get-tuple-element.12.refs_0_, bf16[4,2,64,128]{3,2,1,0:T(8,128)(2,1)} %get-tuple-element.13.refs_1_, bf16[2,512,128]{2,1,0:T(8,128)(2,1)} %get-tuple-element.14.refs_2_, ...), custom_call_target="tpu_custom_call" | custom-call | tf_op jit(solution)/shard_map/pallas_call | solution.py:704

commit v7 on v6

--- a/solution.py
+++ b/solution.py
@@ -60,6 +60,10 @@
         zb = lax.div(self.slab, PY)
         self.has_y = {1: lane < PY - 1, -1: lane > 0}
         self.has_z = {1: zb < nz * ny * 2 // PY - 1, -1: zb > 0}
+        ring = lambda d, n: min(d % n, n - d % n)
+        steps = [(dy, dx) for dy in range(ny) for dx in range(nx) if (dy, dx) != (0, 0)]
+        self.plane_far = sorted(steps, key=lambda s: -ring(s[0], ny) - ring(s[1], nx))
+        self.z_far = sorted(range(1, nz), key=lambda d: -ring(d, nz))
 
     def has(self, dz, dy):
         if dz == 0:
@@ -74,10 +78,12 @@
     def pair(self):
         return (self.slab + 1 - 2 * self.core, self.x)
 
-    def in_plane(self, k):
-        p = lax.rem(self.p + k, self.plane)
-        y, x = lax.div(p, self.nx), lax.rem(p, self.nx)
-        return p, ((self.z * self.ny + y) * 2 + self.core, x)
+    def in_plane(self, step):
+        y, x = lax.rem(self.y + step[0], self.ny), lax.rem(self.x + step[1], self.nx)
+        return y * self.nx + x, ((self.z * self.ny + y) * 2 + self.core, x)
+
+    def back_in_plane(self, step):
+        return self.in_plane((self.ny - step[0], self.nx - step[1]))[0]
 
     def along_z(self, k):
         z = lax.rem(self.z + k, self.nz)
@@ -110,27 +116,28 @@
     def start_plane(self):
         at, r = self.at, self.r
         self.c0.wait_recv()
-        self.s0[...] = (self.v[at.core].astype(F32) + self.r0[...].astype(F32)).astype(BF16)
         self.c1 = []
-        for k in range(1, at.plane):
-            p, device = at.in_plane(k)
+        for k, step in enumerate(at.plane_far):
+            p, device = at.in_plane(step)
             rows = pl.ds(pl.multiple_of(p * r, 16), r)
+            self.s0[rows, :] = (self.v[at.core, rows, :].astype(F32) + self.r0[rows, :].astype(F32)).astype(BF16)
             self.c1.append(
-                self.go(remote(self.s0.at[rows], self.r1.at[k - 1], self.plane_send.at[k - 1], self.plane_recv.at[k - 1], device))
+                self.go(remote(self.s0.at[rows], self.r1.at[k], self.plane_send.at[k], self.plane_recv.at[k], device))
             )
 
     def start_z(self):
         at, r = self.at, self.r
-        total = self.s0[pl.ds(pl.multiple_of(at.p * r, 16), r), :].astype(F32)
-        for k, c in enumerate(self.c1):
-            c.wait_recv()
+        rows = pl.ds(pl.multiple_of(at.p * r, 16), r)
+        total = self.v[at.core, rows, :].astype(F32) + self.r0[rows, :].astype(F32)
+        for k in reversed(range(at.plane - 1)):
+            self.c1[k].wait_recv()
             total = total + self.r1[k].astype(F32)
         self.s1[...] = total.astype(BF16)
         self.r2[at.z] = self.s1[...]
         self.c2 = []
-        for k in range(1, at.nz):
+        for k, step in enumerate(at.z_far):
             self.c2.append(
-                self.go(remote(self.s1, self.r2.at[at.z], self.z_send.at[k - 1], self.z_recv.at[k - 1], at.along_z(k)))
+                self.go(remote(self.s1, self.r2.at[at.z], self.z_send.at[k], self.z_recv.at[k], at.along_z(step)))
             )
 
     def start_back(self):
@@ -143,23 +150,19 @@
         rows = pl.ds(pl.multiple_of(at.p * r, 16), r)
         self.g[at.core, rows, :] = total.astype(BF16)
         self.c3 = []
-        for k in range(1, at.plane):
-            _, device = at.in_plane(k)
-            self.c3.append(
-                self.go(
-                    remote(
-                        self.g.at[at.core, rows], self.g.at[at.core, rows], self.back_send.at[k - 1], self.back_recv.at[k - 1], device
-                    )
-                )
-            )
+        piece = self.g.at[at.core, rows]
+        for k, step in enumerate(at.plane_far):
+            _, device = at.in_plane(step)
+            self.c3.append(self.go(remote(piece, piece, self.back_send.at[k], self.back_recv.at[k], device)))
 
     def start_share(self):
         at, r = self.at, self.r
         self.c4 = []
-        for k in range(at.plane):
-            if k:
-                self.c3[k - 1].wait_recv()
-            p = lax.rem(at.p + at.plane - k, at.plane)
+        for k in reversed(range(at.plane)):
+            p = at.p
+            if k < at.plane - 1:
+                self.c3[k].wait_recv()
+                p = at.back_in_plane(at.plane_far[k])
             piece = self.g.at[at.core, pl.ds(pl.multiple_of(p * r, 16), r)]
             self.c4.append(self.go(remote(piece, piece, self.share_send.at[k], self.share_recv.at[k], at.pair())))
 
@@ -204,24 +207,25 @@
     nz, ny, nx = dims
     at = Place(nz, ny, nx)
 
-    barrier = pltpu.get_barrier_semaphore()
-    others = [at.pair()]
-    others += [at.in_plane(k)[1] for k in range(1, at.plane)]
-    others += [at.along_z(k) for k in range(1, nz)]
-    for device in others:
-        pl.semaphore_signal(barrier, inc=1, device_id=device, device_id_type=MESH)
-    for d in DIRS:
-
-        @pl.when(at.has(*d))
-        def _():
-            pl.semaphore_signal(barrier, inc=1, device_id=at.halo(*d), device_id_type=MESH)
-
     loads = [
         pltpu.make_async_copy(src, dst, load_sem.at[i])
         for i, (src, dst) in enumerate(((cot_hbm, cot), (coarse_hbm, coarse), (tw_hbm, tw), (cw_hbm, cw)))
     ]
     for load in loads:
         load.start()
+
+    barrier = pltpu.get_barrier_semaphore()
+    others = [at.pair()]
+    others += [at.in_plane(step)[1] for step in at.plane_far]
+    others += [at.along_z(step) for step in at.z_far]
+    for d in DIRS:
+
+        @pl.when(at.has(*d))
+        def _():
+            pl.semaphore_signal(barrier, inc=1, device_id=at.halo(*d), device_id_type=MESH)
+
+    for device in others:
+        pl.semaphore_signal(barrier, inc=1, device_id=device, device_id_type=MESH)
 
     loads[0].wait()
     wide[...] = cot[...].astype(F32)

time: 52.4 us -> 50.9 us (0.971)
  Pallas kernels: 51.6 us -> 50.2 us
    pallas_call x1, Pallas kernels: 49 us -> 47.6 us  [step(): pl.pallas_call(functools.partial(kernel, (nz, ny, nx), rows_of), out_shap...]
where the time goes in v7:
time: 50.9 us; the launch traced here: 50.8 us
  Pallas kernels  50.2 us (99%)
  between operations  0.64 us (1%)
    pallas_call x1, Pallas kernels, step(): pl.pallas_call(functools.partial(kernel, (nz, ny, nx), rows_of), out_shap...  47.6 us
    pallas_call x1, Pallas kernels, step(): pl.pallas_call(functools.partial(unpack, n_slab * nx), out_shape=(jax.Sha...  2.62 us

profile of v7, /device:TPU:1, one launch (start us, length us, event | category | flops | bytes accessed | tf_op | source)
XLA Modules:
  0.0 50.8 jit_solution(2708579530877141798)
XLA Ops:
  0.6 47.6 %shard_map.75 = (bf16[2048,128]{1,0:T(8,128)(2,1)}, bf16[4,2,64,128]{3,2,1,0:T(8,128)(2,1)}, bf16[2,512,128]{2,1,0:T(8,128)(2,1)}, bf16[2,1024,128]{2,1,0:T(8,128)(2,1)}) custom-call(bf16[4,2,64,128]{3,2,1,0:T(8,128)(2,1)} %bitcast.18, bf16[1728,128]{1,0:T(8,128)(2,1)} %bitcast.16, bf16[1728,64]{1,0:T(8,128)(2,1)} %bitcast.17, bf16[2048,128]{1,0:T(8,128)(2,1)} %bitcast.14), custom_call_target="tpu_custom_call" | custom-call | flops 7000000000 | bytes 4000000 | tf_op jit(solution)/shard_map/pallas_call | solution.py:686
  48.2 2.6 %shard_map.76 = (bf16[2048,128]{1,0:T(8,128)(2,1)}, bf16[4,2,64,128]{3,2,1,0:T(8,128)(2,1)}, f32[27,64,64]{2,1,0:T(8,128)}, f32[1728,128]{1,0:T(8,128)}) custom-call(bf16[2048,128]{1,0:T(8,128)(2,1)} %get-tuple-element.12.refs_0_, bf16[4,2,64,128]{3,2,1,0:T(8,128)(2,1)} %get-tuple-element.13.refs_1_, bf16[2,512,128]{2,1,0:T(8,128)(2,1)} %get-tuple-element.14.refs_2_, ...), custom_call_target="tpu_custom_call" | custom-call | tf_op jit(solution)/shard_map/pallas_call | solution.py:708

commit v8 on v7

--- a/solution.py
+++ b/solution.py
@@ -437,30 +437,6 @@
         put_cot(z + 1, 0, cot_halo[(0, 1)][z])
         put_cot(z + 1, 5, cot_halo[(0, -1)][z])
 
-    for half in range(2):
-        for q in (0, 9):
-            gh[half, q * C : q * C + C, :] = jnp.zeros((C, 256), BF16)
-
-    def grad_plane(z):
-        partial = dot(w2[...], bb[pl.ds(z * 192, 576), :])
-        for y in range(4):
-            ga = partial[:C, (y + 2) * 128 : (y + 3) * 128]
-            ga = ga + partial[C : 2 * C, (y + 1) * 128 : (y + 2) * 128]
-            ga = ga + partial[2 * C :, y * 128 : y * 128 + 128]
-            gh[y % 2, (z + 1) * C : (z + 2) * C, y // 2 * 128 : y // 2 * 128 + 128] = (
-                ga * ds[z, :, y * 128 : y * 128 + 128]
-            ).astype(BF16)
-
-    unrolled(1, 7)(grad_plane)
-    arrived(cot_copy, FAR)
-    for dz, ze in ((1, 0), (-1, 9)):
-        put_cot(ze, 0, cot_halo[(dz, 1)][0])
-        for y in range(4):
-            put_cot(ze, y + 1, cot_halo[(dz, 0)][0, :, y * 128 : y * 128 + 128])
-        put_cot(ze, 5, cot_halo[(dz, -1)][0])
-    grad_plane(0)
-    grad_plane(7)
-
     def picks(shape, f_dim):
         f = lax.broadcasted_iota(jnp.int32, shape, f_dim)
         c = lax.broadcasted_iota(jnp.int32, shape, 1 - f_dim)
@@ -475,13 +451,43 @@
         return out.astype(BF16)
 
     pick = picks((256, 384), 0)
+
+    def put_picked(planes):
+        for half in range(2):
+            some = dot(gh[half, (planes[0] + 1) * C : (planes[-1] + 2) * C, :], pick).astype(BF16)
+            for n, z in enumerate(planes):
+                for kx in range(3):
+                    cols[z % 2, half, kx * C : (kx + 1) * C, z // 2 * 128 : z // 2 * 128 + 128] = some[
+                        n * C : (n + 1) * C, kx * 128 : kx * 128 + 128
+                    ]
+
     for half in range(2):
-        some = dot(gh[half, C : 9 * C, :], pick).astype(BF16)
-        for z in range(8):
-            for kx in range(3):
-                cols[z % 2, half, kx * C : (kx + 1) * C, z // 2 * 128 : z // 2 * 128 + 128] = some[
-                    z * C : (z + 1) * C, kx * 128 : kx * 128 + 128
-                ]
+        for q in (0, 9):
+            gh[half, q * C : q * C + C, :] = jnp.zeros((C, 256), BF16)
+
+    def grad_plane(z):
+        partial = dot(w2[...], bb[pl.ds(z * 192, 576), :])
+        for y in range(4):
+            ga = partial[:C, (y + 2) * 128 : (y + 3) * 128]
+            ga = ga + partial[C : 2 * C, (y + 1) * 128 : (y + 2) * 128]
+            ga = ga + partial[2 * C :, y * 128 : y * 128 + 128]
+            gh[y % 2, (z + 1) * C : (z + 2) * C, y // 2 * 128 : y // 2 * 128 + 128] = (
+                ga * ds[z, :, y * 128 : y * 128 + 128]
+            ).astype(BF16)
+
+    unrolled(1, 7)(grad_plane)
+    put_picked(range(1, 7))
+    arrived(cot_copy, FAR)
+    for dz, ze in ((1, 0), (-1, 9)):
+        put_cot(ze, 0, cot_halo[(dz, 1)][0])
+        for y in range(4):
+            put_cot(ze, y + 1, cot_halo[(dz, 0)][0, :, y * 128 : y * 128 + 128])
+        put_cot(ze, 5, cot_halo[(dz, -1)][0])
+    grad_plane(0)
+    grad_plane(7)
+    put_picked([0])
+    put_picked([7])
+
 
     def cells(z, y):
         if z < 4 and y < 2:
@@ -604,8 +610,11 @@
         pltpu.make_async_copy(src, dst, sems.at[4 + i])
         for i, (src, dst) in enumerate(zip((held[0], held[1], gcw, gtw), outs))
     ]
-    for i in (2, 3, 0, 1):
-        loads[i].start()
+    for load in loads:
+        load.start()
+    for i in range(2):
+        loads[i].wait()
+        stores[i].start()
     conv, tconv = held[2:]
     loads[2].wait()
     conv_scale = 1.0 / math.sqrt(n_dev * 8 * 4 * 128)
@@ -623,9 +632,6 @@
     tconv_scale = 1.0 / math.sqrt(n_dev * 4 * 2 * 64)
     gtw[...] = tconv[...].reshape(-1, 128)[:1728].astype(F32) * tconv_scale
     stores[3].start()
-    for i in range(2):
-        loads[i].wait()
-        stores[i].start()
     for store in stores:
         store.wait()
 

time: 50.9 us -> 50.9 us (level)
  no operation moved by 1% of the time
where the time goes in v8:
time: 50.9 us; the launch traced here: 50.8 us
  Pallas kernels  50.2 us (99%)
  between operations  0.64 us (1%)
    pallas_call x1, Pallas kernels, step(): pl.pallas_call(functools.partial(kernel, (nz, ny, nx), rows_of), out_shap...  47.6 us
    pallas_call x1, Pallas kernels, step(): pl.pallas_call(functools.partial(unpack, n_slab * nx), out_shape=(jax.Sha...  2.61 us

profile of v8, /device:TPU:1, one launch (start us, length us, event | category | flops | bytes accessed | tf_op | source)
XLA Modules:
  0.0 50.8 jit_solution(9261005664213990708)
XLA Ops:
  0.6 47.6 %shard_map.75 = (bf16[2048,128]{1,0:T(8,128)(2,1)}, bf16[4,2,64,128]{3,2,1,0:T(8,128)(2,1)}, bf16[2,512,128]{2,1,0:T(8,128)(2,1)}, bf16[2,1024,128]{2,1,0:T(8,128)(2,1)}) custom-call(bf16[4,2,64,128]{3,2,1,0:T(8,128)(2,1)} %bitcast.18, bf16[1728,128]{1,0:T(8,128)(2,1)} %bitcast.16, bf16[1728,64]{1,0:T(8,128)(2,1)} %bitcast.17, bf16[2048,128]{1,0:T(8,128)(2,1)} %bitcast.14), custom_call_target="tpu_custom_call" | custom-call | flops 7000000000 | bytes 4000000 | tf_op jit(solution)/shard_map/pallas_call | solution.py:692
  48.2 2.6 %shard_map.76 = (bf16[2048,128]{1,0:T(8,128)(2,1)}, bf16[4,2,64,128]{3,2,1,0:T(8,128)(2,1)}, f32[27,64,64]{2,1,0:T(8,128)}, f32[1728,128]{1,0:T(8,128)}) custom-call(bf16[2048,128]{1,0:T(8,128)(2,1)} %get-tuple-element.12.refs_0_, bf16[4,2,64,128]{3,2,1,0:T(8,128)(2,1)} %get-tuple-element.13.refs_1_, bf16[2,512,128]{2,1,0:T(8,128)(2,1)} %get-tuple-element.14.refs_2_, ...), custom_call_target="tpu_custom_call" | custom-call | tf_op jit(solution)/shard_map/pallas_call | solution.py:714

commit v9 on v8

--- a/solution.py
+++ b/solution.py
@@ -428,7 +428,6 @@
             ],
             axis=1,
         ).astype(BF16)
-    conv_sum.start_plane()
 
     arrived(cot_copy, NEAR)
 
@@ -436,6 +435,8 @@
     def _(z):
         put_cot(z + 1, 0, cot_halo[(0, 1)][z])
         put_cot(z + 1, 5, cot_halo[(0, -1)][z])
+
+    conv_sum.start_plane()
 
     def picks(shape, f_dim):
         f = lax.broadcasted_iota(jnp.int32, shape, f_dim)
@@ -451,6 +452,7 @@
         return out.astype(BF16)
 
     pick = picks((256, 384), 0)
+    pick_t = picks((384, 256), 1)
 
     def put_picked(planes):
         for half in range(2):
@@ -515,7 +517,6 @@
     fill(gt_v, at.plane * rows_of[1], [by_tap[kz, ky] for kz in range(3) for ky in range(3)])
     tconv_sum.start_pair()
 
-    pick_t = picks((384, 256), 1)
     for half in range(2):
         et[half] = dot_nt(pick_t, gh[half]).astype(BF16)
 

time: 50.9 us -> 50.9 us (level)
  no operation moved by 1% of the time
where the time goes in v9:
time: 50.9 us; the launch traced here: 50.8 us
  Pallas kernels  50.1 us (98%)
  between operations  0.64 us (1%)
    pallas_call x1, Pallas kernels, step(): pl.pallas_call(functools.partial(kernel, (nz, ny, nx), rows_of), out_shap...  47.5 us
    pallas_call x1, Pallas kernels, step(): pl.pallas_call(functools.partial(unpack, n_slab * nx), out_shape=(jax.Sha...  2.61 us

profile of v9, /device:TPU:1, one launch (start us, length us, event | category | flops | bytes accessed | tf_op | source)
XLA Modules:
  0.0 50.8 jit_solution(17490901678010026391)
XLA Ops:
  0.6 47.5 %shard_map.75 = (bf16[2048,128]{1,0:T(8,128)(2,1)}, bf16[4,2,64,128]{3,2,1,0:T(8,128)(2,1)}, bf16[2,512,128]{2,1,0:T(8,128)(2,1)}, bf16[2,1024,128]{2,1,0:T(8,128)(2,1)}) custom-call(bf16[4,2,64,128]{3,2,1,0:T(8,128)(2,1)} %bitcast.18, bf16[1728,128]{1,0:T(8,128)(2,1)} %bitcast.16, bf16[1728,64]{1,0:T(8,128)(2,1)} %bitcast.17, bf16[2048,128]{1,0:T(8,128)(2,1)} %bitcast.14), custom_call_target="tpu_custom_call" | custom-call | flops 7000000000 | bytes 4000000 | tf_op jit(solution)/shard_map/pallas_call | solution.py:693
  48.2 2.6 %shard_map.76 = (bf16[2048,128]{1,0:T(8,128)(2,1)}, bf16[4,2,64,128]{3,2,1,0:T(8,128)(2,1)}, f32[27,64,64]{2,1,0:T(8,128)}, f32[1728,128]{1,0:T(8,128)}) custom-call(bf16[2048,128]{1,0:T(8,128)(2,1)} %get-tuple-element.12.refs_0_, bf16[4,2,64,128]{3,2,1,0:T(8,128)(2,1)} %get-tuple-element.13.refs_1_, bf16[2,512,128]{2,1,0:T(8,128)(2,1)} %get-tuple-element.14.refs_2_, ...), custom_call_target="tpu_custom_call" | custom-call | tf_op jit(solution)/shard_map/pallas_call | solution.py:715
